TPU v7x, 128 devices: a whole 4x4x4 slice. The times are simulated.
128 devices in a mesh: pages: 32 (over y, x, core), rep: 4 (over z).
Axes of the slice: x: 4, y: 4, z: 4, core: 2. Of those that a mesh axis runs over, the one named last changes fastest.
Arguments:
- features: bfloat16 [1280, 256, 1152], P('pages'), may hold values from -6 to 6
- queries: bfloat16 [512, 32, 128], P(('pages', 'rep')), may hold values from -6 to 6
- proj_weight: bfloat16 [1152, 128], replicated, may hold values from -0.1875 to 0.1875
- page_ids: int32 [512, 16], P(('pages', 'rep')), may hold values from 0 to 1279, as said below
Outputs:
- scores: float32 [512, 16], P(('pages', 'rep'))
- grad_query: float32 [512, 32, 128], P(('pages', 'rep'))
- grad_proj: float32 [1152, 128], replicated
Inputs may be any that keep to these rules, and one draw needn't show every extreme that they name: `page_ids`: page ids k * 40 to (k + 1) * 40 - 1 form owner range k. Among the 64 entries of the queries of one device (an aligned block of 4 queries), at most 8 fall in one owner range; in every draw some owner ranges receive exactly 8 from every such block.
All inputs are finite; a program needn't handle non-finite values.
Results may differ from a plain program's by a relative error of at most 0.0045.
The roundings to bfloat16 on the way count: a program that leaves them out, or rounds other values in their place, can miss the bound.
Values may be sent and summed in bfloat16 or wider, within the bound.
No kernel may reach another device: no remote copies, remote signals or barrier semaphores. Data moves between devices by JAX's collectives and lax.ppermute only.
A program may use at most 256 MiB of HBM per device.

v0:
```python
import jax
import jax.numpy as jnp
from jax import lax
from jax.sharding import PartitionSpec as P

epsilon = 1e-06
smoothing = 0.05


def unit_rows(values):
    scale = lax.rsqrt(jnp.sum(values * values, axis=-1, keepdims=True) + epsilon)
    return (values * scale, scale)


def unit_backward(values, scale, upstream):
    inner = jnp.sum(values * upstream, axis=-1, keepdims=True)
    return upstream * scale - values * scale**3 * inner


def smooth_forward(query_block, page_block):
    sims = jnp.einsum("stf,sjf->stj", query_block, page_block, preferred_element_type=jnp.float32)
    totals = jnp.sum(jnp.exp(sims / smoothing), axis=2)
    return jnp.sum(smoothing * jnp.log(totals), axis=1)


def smooth_backward(query_block, page_block, weight_col):
    sims = jnp.einsum("stf,sjf->stj", query_block, page_block, preferred_element_type=jnp.float32)
    expw = jnp.exp(sims / smoothing)
    totals = jnp.sum(expw, axis=2, keepdims=True)
    sim_grad = (weight_col[:, None, None] * (expw / totals)).astype(jnp.bfloat16)
    query_grad = jnp.einsum(
        "stj,sjf->stf", sim_grad, page_block, preferred_element_type=jnp.float32
    )
    page_grad = jnp.einsum(
        "stj,stf->sjf", sim_grad, query_block, preferred_element_type=jnp.float32
    )
    return (query_grad, page_grad)


def per_device(features, queries, proj_weight, page_ids):
    owners = lax.axis_size("pages")
    page_count, page_tokens, feat_width = features.shape
    query_count, query_tokens, proj_width = queries.shape
    listed = page_ids.shape[1]
    capacity = 2 * query_count
    pair_count = query_count * listed
    slot_total = capacity * owners
    query_flat = query_tokens * proj_width
    page_flat = page_tokens * proj_width
    flat_ids = page_ids.reshape(pair_count)
    owner_of = flat_ids // page_count
    local_page = flat_ids % page_count
    owner_hits = (owner_of[:, None] == jnp.arange(owners, dtype=jnp.int32)[None, :]).astype(
        jnp.int32
    )
    rank_of = jnp.sum(jnp.cumsum(owner_hits, axis=0) * owner_hits, axis=1) - 1
    position = rank_of * owners + owner_of
    dispatch = jnp.arange(slot_total, dtype=jnp.int32)[:, None] == position[None, :]
    slot_pages = (
        jnp.sum(dispatch.astype(jnp.int32) * (local_page + 1)[None, :], axis=1) - 1
    ).reshape(capacity, owners)
    slot_query = jnp.any(dispatch.reshape(slot_total, query_count, listed), axis=2)
    query_wide = queries.astype(jnp.float32)
    query_unit, query_scale = unit_rows(query_wide)
    query_emb = query_unit.astype(jnp.bfloat16).reshape(query_count, query_flat)
    query_slots = jnp.dot(
        slot_query.astype(jnp.bfloat16), query_emb, preferred_element_type=jnp.float32
    )
    query_slots = query_slots.astype(jnp.bfloat16).reshape(capacity, owners, query_flat)
    rows = features.reshape(page_count * page_tokens, feat_width)
    projected = jnp.dot(rows, proj_weight, preferred_element_type=jnp.float32)
    page_unit, page_scale = unit_rows(projected)
    page_emb = page_unit.astype(jnp.bfloat16).reshape(page_count, page_tokens, proj_width)

    def pick_pages(slot_col):
        return page_emb[jnp.maximum(slot_col, 0)]

    recv_queries, recv_pages = (
        lax.all_to_all(query_slots, "pages", split_axis=1, concat_axis=1, tiled=True),
        lax.all_to_all(slot_pages, "pages", split_axis=1, concat_axis=1, tiled=True),
    )

    def column(item):
        query_col, slot_col, source_col = item

        def column_work(operand):
            page_block = pick_pages(slot_col)
            return smooth_forward(query_col.reshape(owners, query_tokens, proj_width), page_block)

        def column_skip(operand):
            return jnp.zeros((owners,), jnp.float32)

        return lax.cond(jnp.any(slot_col >= 0), column_work, column_skip, 0)

    recv_scores = lax.map(column, (recv_queries, recv_pages, recv_pages))
    score_buf = lax.all_to_all(recv_scores, "pages", split_axis=1, concat_axis=1, tiled=True)
    scores = score_buf.reshape(slot_total)[position].reshape(query_count, listed)
    exp_scores = jnp.exp(scores)
    probability = exp_scores / jnp.sum(exp_scores, axis=1, keepdims=True)
    weight_pairs = probability - (jnp.arange(listed) == 0).astype(jnp.float32)[None, :]
    weight_buf = (
        jnp.zeros((slot_total,), jnp.float32).at[position].set(weight_pairs.reshape(pair_count))
    )
    scores, weight_buf = (scores, weight_buf.reshape(capacity, owners))
    recv_weights = lax.all_to_all(weight_buf, "pages", split_axis=1, concat_axis=1, tiled=True)

    def owner_grads(carry, item):
        query_col, slot_col, weight_col = item

        def owner_work(total):
            query_grad, page_grad = smooth_backward(
                query_col.reshape(owners, query_tokens, proj_width),
                pick_pages(slot_col),
                weight_col,
            )
            hits = (jnp.arange(page_count, dtype=jnp.int32)[:, None] == slot_col[None, :]).astype(
                jnp.float32
            )
            total = total + jnp.dot(
                hits, page_grad.reshape(owners, page_flat), precision=lax.Precision.HIGHEST
            )
            return (total, query_grad.reshape(owners, query_flat))

        def owner_skip(total):
            return (total, jnp.zeros((owners, query_flat), jnp.float32))

        return lax.cond(jnp.any(slot_col >= 0), owner_work, owner_skip, carry)

    start = jnp.zeros((page_count, page_flat), jnp.float32)
    page_unit_grad, recv_grads = lax.scan(
        owner_grads, start, (recv_queries, recv_pages, recv_weights)
    )
    query_buf_grad = lax.all_to_all(recv_grads, "pages", split_axis=1, concat_axis=1, tiled=True)
    query_unit_grad = jnp.dot(
        slot_query.astype(jnp.float32).T,
        query_buf_grad.reshape(slot_total, query_flat),
        precision=lax.Precision.HIGHEST,
    )
    grad_query = unit_backward(
        query_wide, query_scale, query_unit_grad.reshape(query_count, query_tokens, proj_width)
    )
    upstream = page_unit_grad.reshape(page_count * page_tokens, proj_width)
    projected_grad = unit_backward(projected, page_scale, upstream).astype(jnp.bfloat16)
    local_term = lax.dot_general(
        rows, projected_grad, (((0,), (0,)), ((), ())), preferred_element_type=jnp.float32
    )
    grad_proj = lax.psum(local_term, ("pages", "rep"))
    return (scores, grad_query, grad_proj)


def solution(mesh):
    in_specs = (
        P("pages", None, None),
        P(("pages", "rep"), None, None),
        P(),
        P(("pages", "rep"), None),
    )
    out_specs = (P(("pages", "rep"), None), P(("pages", "rep"), None, None), P())
    return jax.shard_map(
        per_device, mesh=mesh, in_specs=in_specs, out_specs=out_specs, check_vma=False
    )
```

profile of v0, /device:TPU:1, one launch (start us, length us, event | category | flops | bytes accessed | tf_op | source)
XLA Modules:
  0.0 740.8 jit_solution(8907196809992447655)
XLA Ops:
  10.1 8.6 %all-to-all-start = ((s32[8,32,1]{0,2,1:T(1,128)}), s32[8,32,1]{0,2,1:T(1,128)S(1)}, u32[]{:S(2)}, u32[]{:S(2)}) async-start(s32[8,32,1]{0,2,1:T(1,128)} %copy.42), calls=%async_computation | async-start | bytes 32768 | tf_op jit(solution)/shard_map/all_to_all | solution.py:80
  20.7 12.5 %multiply_reduce_fusion.2 = (f32[10240]{0:T(1024)S(1)}, f32[10240,128]{1,0:T(8,128)}) fusion(bf16[10240,1152]{1,0:T(8,128)(2,1)} %bitcast.67, bf16[1152,128]{1,0:T(8,128)(2,1)S(1)} %copy-done), kind=kOutput, calls=%fused_computation.37 | convolution fusion | flops 3022510080 | bytes 29171712 | tf_op jit(solution)/shard_map/dot_general | solution.py:71
  34.1 2.5 copy.44
  36.6 7.4 %all-to-all-start.1 = ((bf16[8,32,4096]{2,0,1:T(8,128)(2,1)}), bf16[8,32,4096]{2,0,1:T(8,128)(2,1)}, u32[]{:S(2)}, u32[]{:S(2)}) async-start(bf16[8,32,4096]{2,0,1:T(8,128)(2,1)} %copy.44), calls=%async_computation.1 | async-start | bytes 4194304 | tf_op jit(solution)/shard_map/all_to_all | solution.py:79
  44.1 5.8 multiply_convert_fusion.1
  50.5 21.4 %all-to-all-done.1 = bf16[8,32,4096]{2,0,1:T(8,128)(2,1)} async-done(((bf16[8,32,4096]{2,0,1:T(8,128)(2,1)}), bf16[8,32,4096]{2,0,1:T(8,128)(2,1)}, u32[]{:S(2)}, u32[]{:S(2)}) %all-to-all-start.1) | async-done | bytes 2097184 | tf_op jit(solution)/shard_map/all_to_all | solution.py:79
  72.0 4.1 copy.46
  76.0 28.1 %while.25 = (s32[]{:T(128)}, f32[8,32]{1,0:T(8,128)S(1)}, s32[8,32]{1,0:T(8,128)}, bf16[8,32,4096]{2,1,0:T(8,128)(2,1)}, bf16[40,256,128]{2,1,0:T(8,128)(2,1)S(1)}, /*index=5*/s32[]{:T(128)}, s32[]{:T(128)}) while((s32[]{:T(128)}, f32[8,32]{1,0:T(8,128)S(1)}, s32[8,32]{1,0:T(8,128)}, bf16[8,32,4096]{2,1,0:T(8,128)(2,1)}, ...), condition=%wide.region_12.13_spmd, body=%wide.region_6.12_spmd.sunk | while | flops 67635264 | bytes 7615759 | solution.py:95
  78.0 5.9 conditional.4
  79.1 2.2 gather_fusion
  81.3 2.5 fusion.1
  85.9 5.9 conditional.4
  87.0 2.2 gather_fusion
  89.2 2.5 fusion.1
  104.8 39.4 %all-to-all-start.2 = ((f32[8,32,1]{0,2,1:T(1,128)}), f32[8,32,1]{0,2,1:T(1,128)S(1)}, u32[]{:S(2)}, u32[]{:S(2)}) async-start(f32[8,32,1]{0,2,1:T(1,128)} %bitcast.9), calls=%async_computation.2 | async-start | bytes 32768 | tf_op jit(solution)/shard_map/all_to_all | solution.py:96
  144.3 6.8 all-to-all-done.2
  154.2 4.3 all-to-all-start.3
  158.6 7.0 all-to-all-done.3
  166.2 2.7 broadcast_in_dim.58
  168.9 183.7 %while.26 = (s32[]{:T(128)}, f32[40,32768]{1,0:T(8,128)}, f32[8,32,4096]{2,0,1:T(8,128)}, s32[8,32]{1,0:T(8,128)}, f32[8,32]{1,0:T(8,128)}, /*index=5*/bf16[8,32...) while((s32[]{:T(128)}, f32[40,32768]{1,0:T(8,128)}, ...), condition=%wide.region_20.21_spmd, body=%wide.region_15.20_spmd.sunk | while | flops 707793728 | bytes 37754992 | solution.py:130
  168.9 1.8 compare_reduce_fusion.5
  171.4 29.2 %conditional.5 = (f32[40,32768]{1,0:T(8,128)}, f32[1,32,4096]{2,1,0:T(8,128)S(1)}) conditional(s32[]{:T(128)} %convert_element_type.84, f32[40,32768]{1,0:T(8,128)} %get-tuple-element.371, (s32[32]{0:T(128)}, f32[8,32]{1,0:T(8,128)}, s32[]{:T(128)}, bf16[8,32,4096]{2,1,0:T(8,128)(2,1)}, bf16[40,256,128]{2,1,0:T(8,128)(2,1)S(1)}, ...), branch_computations={%region_17.17_spmd, %region_18.19_spmd} | conditional | flops 707793664 | bytes 33560244 | solution.py:127
  173.8 2.2 gather_fusion.1
  175.9 3.4 fusion.4
  179.3 3.8 fusion.6
  184.3 5.0 fusion.7
  189.3 11.3 %convolution_add_fusion = f32[40,32768]{1,0:T(8,128)} fusion(f32[40,32768]{1,0:T(8,128)} %get-tuple-element.130, f32[4,8,256,128]{3,2,1,0:T(8,128)} %bitcast.63, s32[32]{0:T(128)} %get-tuple-element.131), kind=kOutput, calls=%fused_computation.13 | convolution fusion | flops 504628480 | bytes 14680192 | tf_op jit(solution)/shard_map/while/body/eval_jaxpr/cond/branch_1_fun/dot_general | solution.py:119
  201.4 1.6 copy.80
  203.0 10.7 %dynamic_update_slice.11 = f32[8,32,4096]{2,0,1:T(8,128)} dynamic-update-slice(f32[8,32,4096]{2,0,1:T(8,128)} %get-tuple-element.372, f32[1,32,4096]{2,0,1:T(1,128)S(1)} %copy.80, s32[]{:T(128)} %copy.98, s32[]{:T(128)} %constant.108.clone.1..sunk.1, s32[]{:T(128)} %constant.108.clone.1..sunk.1) | dynamic-update-slice | bytes 1048580 | tf_op jit(solution)/shard_map/while/body/jit(dynamic_update_index_in_dim)/dynamic_update_slice | solution.py:130
  213.7 1.8 compare_reduce_fusion.5
  216.2 29.2 %conditional.5 = (f32[40,32768]{1,0:T(8,128)}, f32[1,32,4096]{2,1,0:T(8,128)S(1)}) conditional(s32[]{:T(128)} %convert_element_type.84, f32[40,32768]{1,0:T(8,128)} %get-tuple-element.371, (s32[32]{0:T(128)}, f32[8,32]{1,0:T(8,128)}, s32[]{:T(128)}, bf16[8,32,4096]{2,1,0:T(8,128)(2,1)}, bf16[40,256,128]{2,1,0:T(8,128)(2,1)S(1)}, ...), branch_computations={%region_17.17_spmd, %region_18.19_spmd} | conditional | flops 707793664 | bytes 33560244 | solution.py:127
  218.6 2.2 gather_fusion.1
  220.8 3.4 fusion.4
  224.2 3.8 fusion.6
  229.2 5.0 fusion.7
  234.1 11.3 %convolution_add_fusion = f32[40,32768]{1,0:T(8,128)} fusion(f32[40,32768]{1,0:T(8,128)} %get-tuple-element.130, f32[4,8,256,128]{3,2,1,0:T(8,128)} %bitcast.63, s32[32]{0:T(128)} %get-tuple-element.131), kind=kOutput, calls=%fused_computation.13 | convolution fusion | flops 504628480 | bytes 14680192 | tf_op jit(solution)/shard_map/while/body/eval_jaxpr/cond/branch_1_fun/dot_general | solution.py:119
  246.2 1.6 copy.80
  247.8 10.7 %dynamic_update_slice.11 = f32[8,32,4096]{2,0,1:T(8,128)} dynamic-update-slice(f32[8,32,4096]{2,0,1:T(8,128)} %get-tuple-element.372, f32[1,32,4096]{2,0,1:T(1,128)S(1)} %copy.80, s32[]{:T(128)} %copy.98, s32[]{:T(128)} %constant.108.clone.1..sunk.1, s32[]{:T(128)} %constant.108.clone.1..sunk.1) | dynamic-update-slice | bytes 1048580 | tf_op jit(solution)/shard_map/while/body/jit(dynamic_update_index_in_dim)/dynamic_update_slice | solution.py:130
  258.5 1.8 compare_reduce_fusion.5
  261.9 1.6 copy.80
  263.5 10.7 %dynamic_update_slice.11 = f32[8,32,4096]{2,0,1:T(8,128)} dynamic-update-slice(f32[8,32,4096]{2,0,1:T(8,128)} %get-tuple-element.372, f32[1,32,4096]{2,0,1:T(1,128)S(1)} %copy.80, s32[]{:T(128)} %copy.98, s32[]{:T(128)} %constant.108.clone.1..sunk.1, s32[]{:T(128)} %constant.108.clone.1..sunk.1) | dynamic-update-slice | bytes 1048580 | tf_op jit(solution)/shard_map/while/body/jit(dynamic_update_index_in_dim)/dynamic_update_slice | solution.py:130
  274.2 1.8 compare_reduce_fusion.5
  277.6 1.6 copy.80
  279.2 10.7 %dynamic_update_slice.11 = f32[8,32,4096]{2,0,1:T(8,128)} dynamic-update-slice(f32[8,32,4096]{2,0,1:T(8,128)} %get-tuple-element.372, f32[1,32,4096]{2,0,1:T(1,128)S(1)} %copy.80, s32[]{:T(128)} %copy.98, s32[]{:T(128)} %constant.108.clone.1..sunk.1, s32[]{:T(128)} %constant.108.clone.1..sunk.1) | dynamic-update-slice | bytes 1048580 | tf_op jit(solution)/shard_map/while/body/jit(dynamic_update_index_in_dim)/dynamic_update_slice | solution.py:130
  289.9 1.8 compare_reduce_fusion.5
  293.2 1.6 copy.80
  294.8 10.7 %dynamic_update_slice.11 = f32[8,32,4096]{2,0,1:T(8,128)} dynamic-update-slice(f32[8,32,4096]{2,0,1:T(8,128)} %get-tuple-element.372, f32[1,32,4096]{2,0,1:T(1,128)S(1)} %copy.80, s32[]{:T(128)} %copy.98, s32[]{:T(128)} %constant.108.clone.1..sunk.1, s32[]{:T(128)} %constant.108.clone.1..sunk.1) | dynamic-update-slice | bytes 1048580 | tf_op jit(solution)/shard_map/while/body/jit(dynamic_update_index_in_dim)/dynamic_update_slice | solution.py:130
  305.6 1.8 compare_reduce_fusion.5
  308.9 1.6 copy.80
  310.5 10.7 %dynamic_update_slice.11 = f32[8,32,4096]{2,0,1:T(8,128)} dynamic-update-slice(f32[8,32,4096]{2,0,1:T(8,128)} %get-tuple-element.372, f32[1,32,4096]{2,0,1:T(1,128)S(1)} %copy.80, s32[]{:T(128)} %copy.98, s32[]{:T(128)} %constant.108.clone.1..sunk.1, s32[]{:T(128)} %constant.108.clone.1..sunk.1) | dynamic-update-slice | bytes 1048580 | tf_op jit(solution)/shard_map/while/body/jit(dynamic_update_index_in_dim)/dynamic_update_slice | solution.py:130
  321.2 1.8 compare_reduce_fusion.5
  324.6 1.6 copy.80
  326.2 10.7 %dynamic_update_slice.11 = f32[8,32,4096]{2,0,1:T(8,128)} dynamic-update-slice(f32[8,32,4096]{2,0,1:T(8,128)} %get-tuple-element.372, f32[1,32,4096]{2,0,1:T(1,128)S(1)} %copy.80, s32[]{:T(128)} %copy.98, s32[]{:T(128)} %constant.108.clone.1..sunk.1, s32[]{:T(128)} %constant.108.clone.1..sunk.1) | dynamic-update-slice | bytes 1048580 | tf_op jit(solution)/shard_map/while/body/jit(dynamic_update_index_in_dim)/dynamic_update_slice | solution.py:130
  336.9 1.8 compare_reduce_fusion.5
  341.9 10.7 %dynamic_update_slice.11 = f32[8,32,4096]{2,0,1:T(8,128)} dynamic-update-slice(f32[8,32,4096]{2,0,1:T(8,128)} %get-tuple-element.372, f32[1,32,4096]{2,0,1:T(1,128)S(1)} %copy.80, s32[]{:T(128)} %copy.98, s32[]{:T(128)} %constant.108.clone.1..sunk.1, s32[]{:T(128)} %constant.108.clone.1..sunk.1) | dynamic-update-slice | bytes 1048580 | tf_op jit(solution)/shard_map/while/body/jit(dynamic_update_index_in_dim)/dynamic_update_slice | solution.py:130
  352.6 178.9 %all-to-all-start.4 = ((f32[8,32,4096]{2,0,1:T(8,128)}), f32[8,32,4096]{2,0,1:T(8,128)}, u32[]{:S(2)}, u32[]{:S(2)}) async-start(f32[8,32,4096]{2,0,1:T(8,128)} %get-tuple-element.153), calls=%async_computation.4 | async-start | bytes 8388608 | tf_op jit(solution)/shard_map/all_to_all | solution.py:133
  531.7 6.7 reshape.260
  538.5 5.4 multiply_reduce_fusion.1
  544.0 14.9 %fusion.17 = f32[1152,128]{0,1:T(8,128)} fusion(bf16[10240,1152]{1,0:T(8,128)(2,1)} %bitcast.68, f32[10240,128]{1,0:T(8,128)} %get-tuple-element.247, f32[10240,128]{1,0:T(8,128)S(1)} %copy-done.2, f32[10240]{0:T(1024)S(1)} %multiply_reduce_fusion.1, f32[10240]{0:T(1024)S(1)} %get-tuple-element.236, f32[10240]{0:T(1024)S(1)} %get-tuple-element.237), kind=kOutput, calls=%fused_computation.43 | convolution fusion | flops 3026452480 | bytes 34791424 | tf_op jit(solution)/shard_map/dot_general | solution.py:144
  559.0 155.6 %all-reduce.2.cloned.1.call-done = f32[1152,128]{0,1:T(8,128)} async-done(((f32[1152,128]{0,1:T(8,128)}), f32[1152,128]{0,1:T(8,128)}) %all-reduce.2.cloned.1.call-update) | async-done | bytes 589840 | tf_op jit(solution)/shard_map/psum | solution.py:147
  714.5 2.1 copy.57
  716.6 6.5 copy.54
  723.2 5.6 copy.55
  728.8 4.3 fusion.22
  (147 shorter events, 41.0 us)
Async XLA Ops:
  7.2 13.5 %copy-start = (bf16[1152,128]{1,0:T(8,128)(2,1)S(1)}, bf16[1152,128]{1,0:T(8,128)(2,1)}, u32[]{:S(2)}) copy-start(bf16[1152,128]{1,0:T(8,128)(2,1)} %param.14) | copy-start | bytes 884740
  10.1 26.5 %all-to-all-start = ((s32[8,32,1]{0,2,1:T(1,128)}), s32[8,32,1]{0,2,1:T(1,128)S(1)}, u32[]{:S(2)}, u32[]{:S(2)}) async-start(s32[8,32,1]{0,2,1:T(1,128)} %copy.42), calls=%async_computation | async-start | bytes 32768 | tf_op jit(solution)/shard_map/all_to_all | solution.py:80
  20.6 12.6 %copy-start.6 = (pred[256,4]{0,1:T(4,128)(4,1)}, pred[256,4]{0,1:T(4,128)(4,1)S(1)}, u32[]{:S(2)}) copy-start(pred[256,4]{0,1:T(4,128)(4,1)S(1)} %fusion.23) | copy-start | bytes 3076
  20.7 12.5 %copy-start.4 = (bf16[4,32,128]{2,1,0:T(8,128)(2,1)S(1)}, bf16[4,32,128]{2,1,0:T(8,128)(2,1)}, u32[]{:S(2)}) copy-start(bf16[4,32,128]{2,1,0:T(8,128)(2,1)} %param.13) | copy-start | bytes 98308
  36.6 35.3 %all-to-all-start.1 = ((bf16[8,32,4096]{2,0,1:T(8,128)(2,1)}), bf16[8,32,4096]{2,0,1:T(8,128)(2,1)}, u32[]{:S(2)}, u32[]{:S(2)}) async-start(bf16[8,32,4096]{2,0,1:T(8,128)(2,1)} %copy.44), calls=%async_computation.1 | async-start | bytes 4194304 | tf_op jit(solution)/shard_map/all_to_all | solution.py:79
  104.8 46.3 %all-to-all-start.2 = ((f32[8,32,1]{0,2,1:T(1,128)}), f32[8,32,1]{0,2,1:T(1,128)S(1)}, u32[]{:S(2)}, u32[]{:S(2)}) async-start(f32[8,32,1]{0,2,1:T(1,128)} %bitcast.9), calls=%async_computation.2 | async-start | bytes 32768 | tf_op jit(solution)/shard_map/all_to_all | solution.py:96
  152.1 0.6 copy-start.8
  154.2 11.3 %all-to-all-start.3 = ((f32[8,32,1]{0,2,1:T(1,128)}), f32[8,32,1]{0,2,1:T(1,128)S(1)}, u32[]{:S(2)}, u32[]{:S(2)}) async-start(f32[8,32,1]{0,2,1:T(1,128)} %copy.49), calls=%async_computation.3 | async-start | bytes 32768 | tf_op jit(solution)/shard_map/all_to_all | solution.py:105
  172.1 7.2 copy-start.5
  200.6 0.8 copy-start.3
  216.9 7.2 copy-start.5
  245.4 0.8 copy-start.3
  261.1 0.8 copy-start.3
  276.8 0.8 copy-start.3
  292.4 0.8 copy-start.3
  308.1 0.8 copy-start.3
  323.8 0.8 copy-start.3
  339.5 0.8 copy-start.3
  352.6 364.1 %all-to-all-start.4 = ((f32[8,32,4096]{2,0,1:T(8,128)}), f32[8,32,4096]{2,0,1:T(8,128)}, u32[]{:S(2)}, u32[]{:S(2)}) async-start(f32[8,32,4096]{2,0,1:T(8,128)} %get-tuple-element.153), calls=%async_computation.4 | async-start | bytes 8388608 | tf_op jit(solution)/shard_map/all_to_all | solution.py:133
  531.5 183.1 %all-reduce.2.cloned.1.call-start = ((), (), s32[]{:S(2)}) async-start(), calls=%async_computation.5 | async-start | bytes 1179648 | tf_op jit(solution)/shard_map/psum | solution.py:147
  538.5 5.5 copy-start.2
  723.2 5.7 copy-start.7
  723.2 10.7 %copy-start.1 = (bf16[1152,128]{1,0:T(8,128)(2,1)S(1)}, bf16[1152,128]{1,0:T(8,128)(2,1)}, u32[]{:S(2)}) copy-start(bf16[1152,128]{1,0:T(8,128)(2,1)} %param.14) | copy-start | bytes 884740
Sparse Core Ops, SparseCore 0:
  559.1 155.4 all-reduce.1
where the time goes:
time: 746 us; the launch traced here: 741 us
  starting transfers between devices  239 us (32%)
  waiting for transfers between devices  191 us (26%)
  local copies, waits for them, and re-layouts  159 us (21%)
  matrix products  84.6 us (11%)
  other arithmetic  42 us (6%)
  between operations  14.2 us (2%)
  loops' own time  11.2 us (2%)
    all_to_all x1, starting transfers between devices, per_device(): lax.all_to_all(recv_grads, 'pages', split_axis=1, concat_axis=1, tiled=True)  179 us
    psum x1, waiting for transfers between devices, per_device(): grad_proj = lax.psum(local_term, ('pages', 'rep'))  156 us
    dynamic_update_slice x16, local copies, waits for them, and re-layouts, per_device(): lax.scan(owner_grads, start, (recv_queries, recv_pages, recv_weights))  98.4 us
    all_to_all x1, starting transfers between devices, per_device(): lax.all_to_all(recv_scores, 'pages', split_axis=1, concat_axis=1, tiled=T...  39.4 us
    dot_general x2, matrix products, owner_work(): jnp.dot(hits, page_grad.reshape(owners, page_flat), precision=lax.Precisi...  22.6 us
    all_to_all x1, waiting for transfers between devices, per_device(): lax.all_to_all(query_slots, 'pages', split_axis=1, concat_axis=1, tiled=T...  21.4 us
    dot_general x1, matrix products, per_device(): lax.dot_general(rows, projected_grad, (((0,), (0,)), ((), ())), preferred...  14.9 us
  transfers between devices with their start and end apart: 6, of which 4 were waited for; matrix products, arithmetic and copies ran while one was open for 7% of the time, Pallas kernels for 0%

commit v1 on v0

v1 whole, which is shorter than its diff:
```python
import math

import jax
import jax.numpy as jnp
from jax import lax
from jax.experimental import pallas as pl
from jax.experimental.pallas import tpu as pltpu
from jax.sharding import PartitionSpec as P

epsilon = 1e-06
smoothing = 0.05
exp2_factor = 1.0 / (smoothing * math.log(2.0))
log2_factor = smoothing * math.log(2.0)

f32 = jnp.float32
bf16 = jnp.bfloat16
i32 = jnp.int32

OWNERS = 32
SLOTS = 8
ENTRIES = OWNERS * SLOTS
QBLOCK = 4
LISTED = 16
QTOK = 32
TOKP = 256
PROJ = 128
P_DEV = 40
D_FEAT = 1152
META = 16
QROWS = QBLOCK * QTOK
QSTRIDE = QROWS + META
CHUNK = 8
LANES = CHUNK * QTOK
MAX_CHUNKS = 72
POSITIONS = 640
MIB = 1 << 20


def iota(shape, dim):
    return lax.broadcasted_iota(i32, shape, dim)


def row_to_col(row, n):
    same = iota((n, n), 0) == iota((n, n), 1)
    return jnp.sum(jnp.where(same, jnp.broadcast_to(row, (n, n)), 0.0), axis=1, keepdims=True)


def col_to_row(col, n):
    same = iota((n, n), 0) == iota((n, n), 1)
    return jnp.sum(jnp.where(same, jnp.broadcast_to(col, (n, n)), 0.0), axis=0, keepdims=True)


def contract_first(a, b):
    return lax.dot_general(a, b, (((0,), (0,)), ((), ())), preferred_element_type=f32)


def contract_last(a, b):
    return lax.dot_general(a, b, (((1,), (1,)), ((), ())), preferred_element_type=f32)


def send_kernel(ids_ref, q_ref, out_ref):
    wide = q_ref[...].reshape(QROWS, PROJ).astype(f32)
    scale = lax.rsqrt(jnp.sum(wide * wide, axis=1, keepdims=True) + epsilon)
    emb = (wide * scale).astype(bf16)
    out_ref[:, 0:QROWS, :] = jnp.broadcast_to(emb[None], (OWNERS, QROWS, PROJ))
    ids = ids_ref[...].astype(f32)
    owner = jnp.floor((ids + 0.5) * (1.0 / P_DEV))
    local = ids - owner * P_DEV
    owner_col = jnp.concatenate([row_to_col(owner[q : q + 1], LISTED) for q in range(QBLOCK)], 0)
    local_col = jnp.concatenate([row_to_col(local[q : q + 1], LISTED) for q in range(QBLOCK)], 0)
    pairs = QBLOCK * LISTED
    lane = iota((pairs, 128), 1)
    entry = iota((pairs, 128), 0)
    hit = (owner_col.astype(i32) == lane).astype(f32)
    before = (iota((pairs, pairs), 1) < iota((pairs, pairs), 0)).astype(f32)
    rank = jnp.sum(
        hit * jnp.dot(before, hit, preferred_element_type=f32), axis=1, keepdims=True
    ).astype(i32)
    code = (entry // LISTED) * 2 + (entry % LISTED == 0).astype(i32)
    value = jnp.where(
        rank == lane,
        local_col + 1.0,
        jnp.where(rank + SLOTS == lane, code.astype(f32), 0.0),
    )
    value = jnp.where(lane < 2 * SLOTS, value, 0.0)
    meta = contract_first(hit, value)[0:OWNERS]
    out_ref[:, QROWS:QSTRIDE, :] = jnp.broadcast_to(
        meta[:, None, :], (OWNERS, META, PROJ)
    ).astype(bf16)


def send_queries(page_ids, queries):
    return pl.pallas_call(
        send_kernel,
        out_shape=jax.ShapeDtypeStruct((OWNERS, QSTRIDE, PROJ), bf16),
        name="send_queries",
    )(page_ids, queries)


def project_kernel(x_ref, w_ref, proj_ref, emb_ref):
    value = jnp.dot(x_ref[...], w_ref[...], preferred_element_type=f32)
    proj_ref[...] = value
    scale = lax.rsqrt(jnp.sum(value * value, axis=1, keepdims=True) + epsilon)
    emb_ref[...] = (value * scale).astype(bf16)


def project(rows, weight):
    total = rows.shape[0]
    block = 512
    return pl.pallas_call(
        project_kernel,
        grid=(total // block,),
        in_specs=[
            pl.BlockSpec((block, D_FEAT), lambda i: (i, 0)),
            pl.BlockSpec((D_FEAT, PROJ), lambda i: (0, 0)),
        ],
        out_specs=[
            pl.BlockSpec((block, PROJ), lambda i: (i, 0)),
            pl.BlockSpec((block, PROJ), lambda i: (i, 0)),
        ],
        out_shape=[
            jax.ShapeDtypeStruct((total, PROJ), f32),
            jax.ShapeDtypeStruct((total, PROJ), bf16),
        ],
        compiler_params=pltpu.CompilerParams(vmem_limit_bytes=32 * MIB),
        cost_estimate=pl.CostEstimate(
            flops=2 * total * D_FEAT * PROJ,
            bytes_accessed=total * (2 * D_FEAT + 6 * PROJ),
            transcendentals=0,
        ),
        name="project",
    )(rows, weight)


def slot_columns(recv_ref):
    meta = recv_ref[...].reshape(OWNERS, QSTRIDE, PROJ)[:, QROWS:QSTRIDE, :].astype(f32)
    meta = meta[:, 0:SLOTS, :].reshape(ENTRIES, PROJ)
    lane = iota((ENTRIES, PROJ), 1)
    slot = iota((ENTRIES, PROJ), 0) % SLOTS
    page = jnp.sum(jnp.where(lane == slot, meta, 0.0), axis=1, keepdims=True).astype(i32) - 1
    code = jnp.sum(jnp.where(lane == slot + SLOTS, meta, 0.0), axis=1, keepdims=True).astype(i32)
    query = (iota((ENTRIES, 1), 0) // SLOTS) * QBLOCK + code // 2
    return page, query, code % 2


def plan_entries(page, query):
    valid = page >= 0
    page_f = page.astype(f32)
    page_row = col_to_row(page_f, ENTRIES)
    earlier = iota((ENTRIES, ENTRIES), 1) < iota((ENTRIES, ENTRIES), 0)
    rank = jnp.sum(
        jnp.where((page_f == page_row) & earlier, 1.0, 0.0), axis=1, keepdims=True
    )
    lane = iota((ENTRIES, 128), 1)
    on_page = (page == lane).astype(f32)
    count = jnp.sum(on_page, axis=0, keepdims=True)
    chunks = jnp.floor((count + (CHUNK - 1)) * (1.0 / CHUNK))
    upper = (iota((128, 128), 0) < iota((128, 128), 1)).astype(f32)
    start = jnp.dot(jnp.broadcast_to(chunks, (8, 128)), upper, preferred_element_type=f32)[0:1]
    position = jnp.sum(on_page * start, axis=1, keepdims=True) * CHUNK + rank
    position = jnp.where(valid, position, -1.0).astype(i32)
    at = position == iota((ENTRIES, POSITIONS), 1)
    entry_id = iota((ENTRIES, 1), 0)
    slot_row = jnp.sum(jnp.where(at, entry_id - ENTRIES, 0), axis=0, keepdims=True) + ENTRIES
    row_of = (query // QBLOCK) * QSTRIDE + (query % QBLOCK) * QTOK
    row_row = jnp.sum(jnp.where(at, row_of, 0), axis=0, keepdims=True)
    query_row = jnp.sum(jnp.where(at, query * QTOK, 0), axis=0, keepdims=True)
    start_col = row_to_col(start, 128)[0:P_DEV]
    chunk_page = (
        jnp.sum(
            jnp.where(start_col <= iota((P_DEV, 128), 1).astype(f32), 1, 0), axis=0, keepdims=True
        )
        - 1
    ) * TOKP
    total = jnp.sum(chunks, axis=1, keepdims=True).astype(i32)
    pad = jnp.zeros((1, POSITIONS - 256), i32)
    last = jnp.concatenate(
        [chunk_page, jnp.broadcast_to(total, (1, 128)), pad], axis=1
    )
    return jnp.concatenate(
        [slot_row, row_row, query_row, last, jnp.zeros((4, POSITIONS), i32)], axis=0
    )


def load_queries(recv_ref, table_ref, chunk):
    parts = []
    for j in range(CHUNK):
        row = pl.multiple_of(table_ref[1, chunk * CHUNK + j], 16)
        parts.append(recv_ref[pl.ds(row, QTOK), :])
    return jnp.concatenate(parts, axis=0)


def load_page(emb_ref, table_ref, chunk):
    return emb_ref[pl.ds(pl.multiple_of(table_ref[3, chunk], TOKP), TOKP), :]


def forward_kernel(recv_ref, emb_ref, back_ref, table_out, logs_ref, exps_ref, table_ref, logs_of, sem):
    page, query, positive = slot_columns(recv_ref)
    table_out[...] = plan_entries(page, query)
    copy = pltpu.make_async_copy(table_out, table_ref, sem)
    copy.start()
    copy.wait()
    group = iota((1, 128), 1) // QTOK

    def pair(step, carry):
        for u in range(2):
            chunk = 2 * step + u
            sims = contract_last(
                load_page(emb_ref, table_ref, chunk), load_queries(recv_ref, table_ref, chunk)
            )
            logs = jnp.log2(jnp.sum(jnp.exp2(sims * exp2_factor), axis=0, keepdims=True))
            logs_ref[pl.ds(chunk, 1), :] = logs
            for j in range(CHUNK):
                tile = logs[:, (j // 4) * 128 : (j // 4) * 128 + 128]
                slot = table_ref[0, chunk * CHUNK + j]
                logs_of[pl.ds(slot, 1), :] = jnp.where(group == j % 4, tile, 0.0)
        return carry

    lax.fori_loop(0, (table_ref[3, 128] + 1) // 2, pair, 0)
    scores = log2_factor * jnp.sum(logs_of[0:ENTRIES, :], axis=1, keepdims=True)
    valid = page >= 0
    exps = jnp.where(valid, jnp.exp(scores), 0.0)
    exps_ref[...] = jnp.broadcast_to(exps, (ENTRIES, 128))
    lane = iota((ENTRIES, 128), 1)
    sums = jnp.sum(jnp.where(query == lane, exps, 0.0), axis=0, keepdims=True)
    slot = iota((ENTRIES, 128), 0) % SLOTS
    spread = jnp.where((lane == slot) & valid, scores, 0.0).reshape(OWNERS, SLOTS, 128)
    spread = jnp.sum(spread, axis=1, keepdims=True)
    which = iota((OWNERS, SLOTS, 128), 1)
    back_ref[...] = jnp.where(
        which == 0, sums[None], jnp.where(which == 1, spread, 0.0)
    )


def forward(recv, emb):
    return pl.pallas_call(
        forward_kernel,
        out_shape=[
            jax.ShapeDtypeStruct((OWNERS, SLOTS, 128), f32),
            jax.ShapeDtypeStruct((8, POSITIONS), i32),
            jax.ShapeDtypeStruct((MAX_CHUNKS, LANES), f32),
            jax.ShapeDtypeStruct((ENTRIES, 128), f32),
        ],
        scratch_shapes=[
            pltpu.SMEM((8, POSITIONS), i32),
            pltpu.VMEM((ENTRIES + 8, 128), f32),
            pltpu.SemaphoreType.DMA,
        ],
        compiler_params=pltpu.CompilerParams(vmem_limit_bytes=32 * MIB),
        name="forward",
    )(recv, emb)


FEAT_PAGES = 4
FEAT_ROWS = FEAT_PAGES * TOKP
FEAT_STEPS = P_DEV // FEAT_PAGES


def backward_kernel(
    table_ref, recv_ref, emb_ref, logs_ref, exps_ref, sums_ref, proj_hbm, feat_hbm,
    query_out, grad_out, weight_of, page_acc, query_acc, proj_ref, feat_ref, sems,
):
    def feature_copy(step):
        part = pl.ds(step * FEAT_ROWS, FEAT_ROWS)
        return pltpu.make_async_copy(feat_hbm.at[part], feat_ref.at[part], sems.at[step])

    proj_copy = pltpu.make_async_copy(proj_hbm, proj_ref, sems.at[FEAT_STEPS])
    proj_copy.start()
    for step in range(FEAT_STEPS):
        feature_copy(step).start()

    page, query, positive = slot_columns(recv_ref)
    sums = jnp.sum(sums_ref[...], axis=0)[0:1]
    lane = iota((ENTRIES, 128), 1)
    total = jnp.sum(jnp.where(query == lane, sums, 0.0), axis=1, keepdims=True)
    valid = page >= 0
    total = jnp.where(valid, total, 1.0)
    weight_of[0:ENTRIES, :] = jnp.where(
        valid, exps_ref[...] / total - positive.astype(f32), 0.0
    )
    weight_of[ENTRIES : ENTRIES + 8, :] = jnp.zeros((8, 128), f32)
    page_acc[...] = jnp.zeros(page_acc.shape, f32)
    query_acc[...] = jnp.zeros(query_acc.shape, f32)
    group = iota((1, 128), 1) // QTOK

    def pair(step, carry):
        results = []
        for u in range(2):
            chunk = 2 * step + u
            tokens = load_page(emb_ref, table_ref, chunk)
            queries = load_queries(recv_ref, table_ref, chunk)
            weights = []
            for half in range(CHUNK // 4):
                tile = jnp.zeros((1, 128), f32)
                for j in range(4):
                    slot = table_ref[0, chunk * CHUNK + half * 4 + j]
                    tile = jnp.where(group == j, weight_of[pl.ds(slot, 1), :], tile)
                weights.append(tile)
            weights = jnp.concatenate(weights, axis=1)
            sims = contract_last(tokens, queries)
            share = jnp.exp2(sims * exp2_factor - logs_ref[pl.ds(chunk, 1), :])
            sim_grad = (share * weights).astype(bf16)
            page_part = jnp.dot(sim_grad, queries, preferred_element_type=f32)
            query_part = contract_first(sim_grad, tokens)
            results.append((chunk, page_part, query_part))
        for chunk, page_part, query_part in results:
            rows = pl.ds(pl.multiple_of(table_ref[3, chunk], TOKP), TOKP)
            page_acc[rows, :] += page_part
            for j in range(CHUNK):
                at = pl.ds(pl.multiple_of(table_ref[2, chunk * CHUNK + j], QTOK), QTOK)
                query_acc[at, :] += query_part[j * QTOK : (j + 1) * QTOK]
        return carry

    lax.fori_loop(0, (table_ref[3, 128] + 1) // 2, pair, 0)
    query_out[...] = query_acc[...].astype(query_out.dtype)
    proj_copy.wait()
    grad_out[...] = jnp.zeros(grad_out.shape, f32)

    def feature_step(step, carry):
        part = pl.ds(pl.multiple_of(step * FEAT_ROWS, FEAT_ROWS), FEAT_ROWS)
        value = proj_ref[part, :]
        upstream = page_acc[part, :]
        scale = lax.rsqrt(jnp.sum(value * value, axis=1, keepdims=True) + epsilon)
        inner = jnp.sum(value * upstream, axis=1, keepdims=True)
        grad = (upstream * scale - value * (scale * scale * scale * inner)).astype(bf16)
        feature_copy(step).wait()
        grad_out[...] += contract_first(feat_ref[part, :], grad)
        return carry

    lax.fori_loop(0, FEAT_STEPS, feature_step, 0)


def backward(table, recv, emb, logs, exps, sums, proj, rows):
    vmem = pl.BlockSpec(memory_space=pltpu.VMEM)
    hbm = pl.BlockSpec(memory_space=pl.ANY)
    return pl.pallas_call(
        backward_kernel,
        in_specs=[pl.BlockSpec(memory_space=pltpu.SMEM), vmem, vmem, vmem, vmem, vmem, hbm, hbm],
        out_specs=[vmem, vmem],
        out_shape=[
            jax.ShapeDtypeStruct((OWNERS * QROWS, PROJ), bf16),
            jax.ShapeDtypeStruct((D_FEAT, PROJ), f32),
        ],
        scratch_shapes=[
            pltpu.VMEM((ENTRIES + 8, 128), f32),
            pltpu.VMEM((P_DEV * TOKP, PROJ), f32),
            pltpu.VMEM((OWNERS * QROWS, PROJ), f32),
            pltpu.VMEM((P_DEV * TOKP, PROJ), f32),
            pltpu.VMEM((P_DEV * TOKP, D_FEAT), bf16),
            pltpu.SemaphoreType.DMA((FEAT_STEPS + 1,)),
        ],
        compiler_params=pltpu.CompilerParams(vmem_limit_bytes=60 * MIB),
        name="backward",
    )(table, recv, emb, logs, exps, sums, proj, rows)


def query_kernel(parts_ref, q_ref, out_ref):
    upstream = jnp.sum(parts_ref[...].astype(f32), axis=0)
    wide = q_ref[...].reshape(QROWS, PROJ).astype(f32)
    scale = lax.rsqrt(jnp.sum(wide * wide, axis=1, keepdims=True) + epsilon)
    inner = jnp.sum(wide * upstream, axis=1, keepdims=True)
    out_ref[...] = (upstream * scale - wide * (scale * scale * scale * inner)).reshape(
        out_ref.shape
    )


def query_grads(parts, queries):
    return pl.pallas_call(
        query_kernel,
        out_shape=jax.ShapeDtypeStruct(queries.shape, f32),
        compiler_params=pltpu.CompilerParams(vmem_limit_bytes=32 * MIB),
        name="query_grads",
    )(parts, queries)


def listed_scores(sums, page_ids):
    owner_of = page_ids.reshape(-1) // P_DEV
    hits = (owner_of[:, None] == jnp.arange(OWNERS, dtype=i32)[None, :]).astype(i32)
    rank_of = jnp.sum(jnp.cumsum(hits, axis=0) * hits, axis=1) - 1
    slots = sums[:, 1, 0:SLOTS]
    pick = (hits != 0)[:, :, None] & (rank_of[:, None] == jnp.arange(SLOTS, dtype=i32))[:, None, :]
    return jnp.sum(jnp.where(pick, slots[None], 0.0), axis=(1, 2)).reshape(page_ids.shape)


def exchange(values, axes):
    return lax.all_to_all(values, axes, split_axis=0, concat_axis=0, tiled=True)


def per_device(features, queries, proj_weight, page_ids):
    everyone = ("pages", "rep")
    devices = lax.axis_size(everyone)
    rows = features.reshape(P_DEV * TOKP, D_FEAT)
    recv = exchange(send_queries(page_ids, queries), "pages").reshape(OWNERS * QSTRIDE, PROJ)
    proj, emb = project(rows, proj_weight)
    back, table, logs, exps = forward(recv, emb)
    sums = exchange(back, "pages")
    query_parts, local_term = backward(table, recv, emb, logs, exps, sums, proj, rows)
    parts = exchange(query_parts.reshape(OWNERS, QROWS, PROJ), "pages")
    grad_query = query_grads(parts, queries)
    scores = listed_scores(sums, page_ids)
    shares = exchange(local_term.astype(bf16).reshape(devices, D_FEAT // devices, PROJ), everyone)
    share = jnp.sum(shares.astype(f32), axis=0).astype(bf16)
    whole = exchange(jnp.broadcast_to(share[None], shares.shape), everyone)
    grad_proj = whole.reshape(D_FEAT, PROJ).astype(f32)
    return (scores, grad_query, grad_proj)


def solution(mesh):
    in_specs = (
        P("pages", None, None),
        P(("pages", "rep"), None, None),
        P(),
        P(("pages", "rep"), None),
    )
    out_specs = (P(("pages", "rep"), None), P(("pages", "rep"), None, None), P())
    return jax.shard_map(
        per_device, mesh=mesh, in_specs=in_specs, out_specs=out_specs, check_vma=False
    )
```

time: 746 us -> 154 us (0.21)
  starting transfers between devices: 239 us -> 17 us
  waiting for transfers between devices: 191 us -> 27.7 us
  local copies, waits for them, and re-layouts: 159 us -> 10.4 us
  matrix products: 84.6 us -> 0 us
  Pallas kernels: 0 us -> 50.8 us
  blocking collectives: 0 us -> 45.3 us
  other arithmetic: 42 us -> 1.75 us
  between operations: 14.2 us -> 0.8 us
  loops' own time: 11.2 us -> 0 us
    all_to_all x5 -> x3, starting transfers between devices: 239 us -> 17 us  [exchange(): return lax.all_to_all(values, axes, split_axis=0, concat_axis=0, tiled=True)]
    psum x1 -> x0, waiting for transfers between devices: 156 us -> none  [per_device(): grad_proj = lax.psum(local_term, ('pages', 'rep'))]
    dynamic_update_slice x24 -> x0, local copies, waits for them, and re-layouts: 98.7 us -> none  [the longest x16 98.4 us: per_device(): lax.scan(owner_grads, start, (recv_queries, recv_pages, recv_weights))]
    dot_general x14 -> x0, matrix products: 84.6 us -> none  [the longest x2 22.6 us: owner_work(): jnp.dot(hits, page_grad.reshape(owners, page_flat), precision=lax.Precisi...]
    pallas_call x0 -> x5, Pallas kernels: none -> 50.8 us  [the longest x1 22.6 us: backward(): pl.pallas_call(backward_kernel, in_specs=[pl.BlockSpec(memory_space=pltpu...]
    all_to_all x0 -> x2, blocking collectives: none -> 45.3 us  [exchange(): return lax.all_to_all(values, axes, split_axis=0, concat_axis=0, tiled=True)]
    reduce_or x17 -> x0, other arithmetic: 25.4 us -> none  [the longest x8 14.8 us: owner_grads(): return lax.cond(jnp.any(slot_col >= 0), owner_work, owner_skip, carry)]
    while x20 -> x0, local copies, waits for them, and re-layouts: 12.4 us -> none
  transfers between devices with their start and end apart: 6 -> 3, of which waited for: 4 -> 2; matrix products, arithmetic and copies ran while one was open for 7% -> 2% of each run, Pallas kernels for 0% -> 13%
where the time goes in v1:
time: 154 us
  Pallas kernels  50.8 us (33%)
  blocking collectives  45.3 us (29%)
  waiting for transfers between devices  27.7 us (18%)
  starting transfers between devices  17 us (11%)
  local copies, waits for them, and re-layouts  10.4 us (7%)
  other arithmetic  1.75 us (1%)
    all_to_all x2, blocking collectives, exchange(): return lax.all_to_all(values, axes, split_axis=0, concat_axis=0, tiled=True)  45.3 us
    all_to_all x3, waiting for transfers between devices, exchange(): return lax.all_to_all(values, axes, split_axis=0, concat_axis=0, tiled=True)  27.7 us
    pallas_call x1, Pallas kernels, backward(): pl.pallas_call(backward_kernel, in_specs=[pl.BlockSpec(memory_space=pltpu...  22.6 us
    pallas_call x1, Pallas kernels, project(): pl.pallas_call(project_kernel, grid=(total // block,), in_specs=[pl.Block...  19.8 us
    all_to_all x3, starting transfers between devices, exchange(): return lax.all_to_all(values, axes, split_axis=0, concat_axis=0, tiled=True)  17 us
    unnamed x20, local copies, waits for them, and re-layouts  6.61 us
    pallas_call x1, Pallas kernels, forward(): pl.pallas_call(forward_kernel, out_shape=[jax.ShapeDtypeStruct((OWNERS, S...  5.08 us
  transfers between devices with their start and end apart: 3, of which 2 were waited for; matrix products, arithmetic and copies ran while one was open for 2% of the time, Pallas kernels for 13%

profile of v1, /device:TPU:1, one launch (start us, length us, event | category | flops | bytes accessed | tf_op | source)
XLA Modules:
  0.0 153.8 jit_solution(1983855672930723210)
XLA Ops:
  0.6 0.0 copy-start.4
  0.6 2.5 %send_queries.1 = bf16[32,144,128]{2,1,0:T(8,128)(2,1)} custom-call(s32[4,16]{1,0:T(4,128)} %ids_ref.1, bf16[4,32,128]{2,1,0:T(8,128)(2,1)} %q_ref.3), custom_call_target="tpu_custom_call" | custom-call | tf_op jit(solution)/shard_map/send_queries/pallas_call | solution.py:93
  3.1 8.6 %all-to-all-start = ((bf16[32,144,128]{2,1,0:T(8,128)(2,1)}), bf16[32,144,128]{2,1,0:T(8,128)(2,1)S(1)}, u32[]{:S(2)}, u32[]{:S(2)}) async-start(bf16[32,144,128]{2,1,0:T(8,128)(2,1)} %send_queries.1), calls=%async_computation | async-start | bytes 2359296 | tf_op jit(solution)/shard_map/all_to_all | solution.py:386
  11.7 0.0 copy-done.4
  11.7 19.8 %project.1 = (f32[10240,128]{1,0:T(8,128)S(1)}, bf16[10240,128]{1,0:T(8,128)(2,1)S(1)}) custom-call(bf16[10240,1152]{1,0:T(8,128)(2,1)} %bitcast.6, bf16[1152,128]{1,0:T(8,128)(2,1)S(1)} %copy-done.4), custom_call_target="tpu_custom_call" | custom-call | flops 3019898880 | bytes 31457280 | tf_op jit(solution)/shard_map/project/pallas_call | solution.py:110
  31.5 0.0 copy-start.1
  31.5 1.5 copy-done.1
  33.0 0.0 copy-start.3
  33.0 2.3 %copy-done.3 = f32[10240,128]{1,0:T(8,128)} copy-done((f32[10240,128]{1,0:T(8,128)}, f32[10240,128]{1,0:T(8,128)S(1)}, u32[]{:S(2)}) %copy-start.3) | copy-done | bytes 5242904
  35.3 0.0 all-to-all-done
  35.3 0.0 copy-start
  35.3 0.0 copy-start.2
  35.3 2.2 %copy-done.2 = bf16[10240,128]{1,0:T(8,128)(2,1)S(1)} copy-done((bf16[10240,128]{1,0:T(8,128)(2,1)S(1)}, bf16[10240,128]{1,0:T(8,128)(2,1)}, u32[]{:S(2)}) %copy-start.2) | copy-done | bytes 2621464
  37.5 5.1 %forward.1 = (f32[32,8,128]{2,1,0:T(8,128)S(1)}, s32[8,640]{1,0:T(8,128)S(1)}, f32[72,256]{1,0:T(8,128)S(1)}, f32[256,128]{1,0:T(8,128)S(1)}) custom-call(bf16[4608,128]{1,0:T(8,128)(2,1)S(1)} %bitcast.4, bf16[10240,128]{1,0:T(8,128)(2,1)S(1)} %copy-done.2), custom_call_target="tpu_custom_call" | custom-call | tf_op jit(solution)/shard_map/forward/pallas_call | solution.py:236
  42.5 0.0 copy-start.5
  42.6 0.6 copy-done.5
  43.2 0.0 copy-start.7
  43.2 0.0 copy-start.8
  43.2 18.1 %all_to_all.25.sums_ref = f32[32,8,128]{2,1,0:T(8,128)} all-to-all(f32[32,8,128]{2,1,0:T(8,128)S(1)} %get-tuple-element.12), channel_id=1, replica_groups=mesh['pages'=32,'rep'=4] {'pages'}, dimensions={0} | all-to-all | bytes 262144 | tf_op jit(solution)/shard_map/all_to_all | solution.py:386
  61.3 0.0 copy-done.7
  61.3 0.0 copy-done.8
  61.3 0.0 copy-done
  61.3 22.6 %backward.1 = (bf16[4096,128]{1,0:T(8,128)(2,1)}, f32[1152,128]{1,0:T(8,128)}) custom-call(s32[8,640]{1,0:T(8,128)} %copy-done.8, bf16[4608,128]{1,0:T(8,128)(2,1)} %bitcast.5, bf16[10240,128]{1,0:T(8,128)(2,1)} %copy-done.1, f32[72,256]{1,0:T(8,128)} %copy-done.7, f32[256,128]{1,0:T(8,128)} %copy-done.5, f32[32,8,128]{2,1,0:T(8,128)} %all_to_all.25.sums_ref, ...), custom_call_target="tpu_custom_call" | custom-call | tf_op jit(solution)/shard_map/backward/pallas_call | solution.py:336
  83.8 0.0 copy-start.9
  83.9 1.1 convert_element_type.19
  85.0 0.1 reshape.101
  85.1 27.3 %all_to_all.26 = bf16[128,9,128]{2,1,0:T(8,128)(2,1)S(1)} all-to-all(bf16[128,9,128]{2,1,0:T(8,128)(2,1)S(1)} %reshape.101), channel_id=1, replica_groups=mesh['pages'=32,'rep'=4] {'pages','rep'}, dimensions={0} | all-to-all | bytes 589824 | tf_op jit(solution)/shard_map/all_to_all | solution.py:386
  112.4 0.1 reduce_sum.32
  112.5 0.0 copy-start.6
  112.5 0.9 broadcast_in_dim.29
  113.4 4.3 %all-to-all-start.4 = ((bf16[128,9,128]{2,1,0:T(8,128)(2,1)}), bf16[128,9,128]{2,1,0:T(8,128)(2,1)S(1)}, u32[]{:S(2)}, u32[]{:S(2)}) async-start(bf16[128,9,128]{2,1,0:T(8,128)(2,1)} %broadcast_in_dim.29), calls=%async_computation.4 | async-start | bytes 1048576 | tf_op jit(solution)/shard_map/all_to_all | solution.py:386
  117.7 0.0 copy-done.9
  117.7 0.1 div.14
  117.8 0.1 and.25
  117.9 13.5 %all-to-all-done.4 = bf16[128,9,128]{2,1,0:T(8,128)(2,1)S(1)} async-done(((bf16[128,9,128]{2,1,0:T(8,128)(2,1)}), bf16[128,9,128]{2,1,0:T(8,128)(2,1)S(1)}, u32[]{:S(2)}, u32[]{:S(2)}) %all-to-all-start.4) | async-done | bytes 294944 | tf_op jit(solution)/shard_map/all_to_all | solution.py:386
  131.4 4.1 %all-to-all-start.2 = ((bf16[32,128,128]{2,1,0:T(8,128)(2,1)}), bf16[32,128,128]{2,1,0:T(8,128)(2,1)S(1)}, u32[]{:S(2)}, u32[]{:S(2)}) async-start(bf16[32,128,128]{2,1,0:T(8,128)(2,1)} %bitcast.3), calls=%async_computation.2 | async-start | bytes 2097152 | tf_op jit(solution)/shard_map/all_to_all | solution.py:386
  135.6 0.1 broadcast_compare_fusion
  135.7 0.1 copy.7
  135.8 0.1 reduce_window_sum.11
  135.9 0.2 select_reduce_fusion.1
  136.1 0.9 slice.4
  137.0 0.1 select_reduce_fusion
  137.1 0.7 reshape.99
  137.8 0.9 reshape.102
  138.7 14.2 %all-to-all-done.2.parts_ref = bf16[32,128,128]{2,1,0:T(8,128)(2,1)S(1)} async-done(((bf16[32,128,128]{2,1,0:T(8,128)(2,1)}), bf16[32,128,128]{2,1,0:T(8,128)(2,1)S(1)}, u32[]{:S(2)}, u32[]{:S(2)}) %all-to-all-start.2) | async-done | bytes 1048608 | tf_op jit(solution)/shard_map/all_to_all | solution.py:386
  152.9 0.0 copy-done.6
  152.9 0.9 query_grads.1
  (5 shorter events, 0.0 us)
Async XLA Ops:
  0.6 11.1 %copy-start.4 = (bf16[1152,128]{1,0:T(8,128)(2,1)S(1)}, bf16[1152,128]{1,0:T(8,128)(2,1)}, u32[]{:S(2)}) copy-start(bf16[1152,128]{1,0:T(8,128)(2,1)} %w_ref.1) | copy-start | bytes 884740
  3.1 32.2 %all-to-all-start = ((bf16[32,144,128]{2,1,0:T(8,128)(2,1)}), bf16[32,144,128]{2,1,0:T(8,128)(2,1)S(1)}, u32[]{:S(2)}, u32[]{:S(2)}) async-start(bf16[32,144,128]{2,1,0:T(8,128)(2,1)} %send_queries.1), calls=%async_computation | async-start | bytes 2359296 | tf_op jit(solution)/shard_map/all_to_all | solution.py:386
  31.5 1.5 copy-start.1
  33.0 2.3 %copy-start.3 = (f32[10240,128]{1,0:T(8,128)}, f32[10240,128]{1,0:T(8,128)S(1)}, u32[]{:S(2)}) copy-start(f32[10240,128]{1,0:T(8,128)S(1)} %get-tuple-element.16.proj_hbm) | copy-start | bytes 15728644
  35.3 26.0 %copy-start = (bf16[32,144,128]{2,1,0:T(8,128)(2,1)}, bf16[32,144,128]{2,1,0:T(8,128)(2,1)S(1)}, u32[]{:S(2)}) copy-start(bf16[32,144,128]{2,1,0:T(8,128)(2,1)S(1)} %all-to-all-done) | copy-start | bytes 3538948
  35.3 2.2 %copy-start.2 = (bf16[10240,128]{1,0:T(8,128)(2,1)S(1)}, bf16[10240,128]{1,0:T(8,128)(2,1)}, u32[]{:S(2)}) copy-start(bf16[10240,128]{1,0:T(8,128)(2,1)} %copy-done.1) | copy-start | bytes 7864324
  42.5 0.7 copy-start.5
  43.2 18.1 %copy-start.7 = (f32[72,256]{1,0:T(8,128)}, f32[72,256]{1,0:T(8,128)S(1)}, u32[]{:S(2)}) copy-start(f32[72,256]{1,0:T(8,128)S(1)} %get-tuple-element.14.logs_ref) | copy-start | bytes 221188
  43.2 18.1 %copy-start.8 = (s32[8,640]{1,0:T(8,128)}, s32[8,640]{1,0:T(8,128)S(1)}, u32[]{:S(2)}) copy-start(s32[8,640]{1,0:T(8,128)S(1)} %get-tuple-element.13.table_ref) | copy-start | bytes 61444
  83.8 33.9 %copy-start.9 = (s32[4,16]{1,0:T(4,128)S(1)}, s32[4,16]{1,0:T(4,128)}, u32[]{:S(2)}) copy-start(s32[4,16]{1,0:T(4,128)} %ids_ref.1) | copy-start | bytes 772
  112.5 40.4 %copy-start.6 = (bf16[4,32,128]{2,1,0:T(8,128)(2,1)S(1)}, bf16[4,32,128]{2,1,0:T(8,128)(2,1)}, u32[]{:S(2)}) copy-start(bf16[4,32,128]{2,1,0:T(8,128)(2,1)} %q_ref.3) | copy-start | bytes 98308
  113.4 18.1 %all-to-all-start.4 = ((bf16[128,9,128]{2,1,0:T(8,128)(2,1)}), bf16[128,9,128]{2,1,0:T(8,128)(2,1)S(1)}, u32[]{:S(2)}, u32[]{:S(2)}) async-start(bf16[128,9,128]{2,1,0:T(8,128)(2,1)} %broadcast_in_dim.29), calls=%async_computation.4 | async-start | bytes 1048576 | tf_op jit(solution)/shard_map/all_to_all | solution.py:386
  131.4 21.4 %all-to-all-start.2 = ((bf16[32,128,128]{2,1,0:T(8,128)(2,1)}), bf16[32,128,128]{2,1,0:T(8,128)(2,1)S(1)}, u32[]{:S(2)}, u32[]{:S(2)}) async-start(bf16[32,128,128]{2,1,0:T(8,128)(2,1)} %bitcast.3), calls=%async_computation.2 | async-start | bytes 2097152 | tf_op jit(solution)/shard_map/all_to_all | solution.py:386

commit v2 on v1

--- a/solution.py
+++ b/solution.py
@@ -31,9 +31,14 @@
 QSTRIDE = QROWS + META
 CHUNK = 8
 LANES = CHUNK * QTOK
-MAX_CHUNKS = 72
+GRAD_ROWS = D_FEAT // OWNERS
+GRAD_PAD = 48
+RSTRIDE = QROWS
 POSITIONS = 640
+EMPTY_CHUNK = POSITIONS // CHUNK - 1
+UNROLL = 4
 MIB = 1 << 20
+SMALL = pltpu.CompilerParams(vmem_limit_bytes=8 * MIB)
 
 
 def iota(shape, dim):
@@ -93,36 +98,68 @@
     return pl.pallas_call(
         send_kernel,
         out_shape=jax.ShapeDtypeStruct((OWNERS, QSTRIDE, PROJ), bf16),
+        compiler_params=SMALL,
         name="send_queries",
     )(page_ids, queries)
 
 
-def project_kernel(x_ref, w_ref, proj_ref, emb_ref):
-    value = jnp.dot(x_ref[...], w_ref[...], preferred_element_type=f32)
-    proj_ref[...] = value
-    scale = lax.rsqrt(jnp.sum(value * value, axis=1, keepdims=True) + epsilon)
-    emb_ref[...] = (value * scale).astype(bf16)
+PROJ_ROWS = 1024
+PROJ_SLOTS = 4
+PROJ_STEPS = P_DEV * TOKP // PROJ_ROWS
+
+
+def project_kernel(x_hbm, w_ref, proj_hbm, emb_hbm, x_ref, proj_ref, emb_ref, sems, proj_sems, emb_sems):
+    def part(step):
+        return pl.ds(step * PROJ_ROWS, PROJ_ROWS)
+
+    def load(step):
+        slot = step % PROJ_SLOTS
+        return pltpu.make_async_copy(x_hbm.at[part(step)], x_ref.at[slot], sems.at[slot])
+
+    def stores(step):
+        return (
+            pltpu.make_async_copy(proj_ref.at[part(step)], proj_hbm.at[part(step)], proj_sems.at[step]),
+            pltpu.make_async_copy(emb_ref.at[part(step)], emb_hbm.at[part(step)], emb_sems.at[step]),
+        )
+
+    for step in range(PROJ_SLOTS):
+        load(step).start()
+    for step in range(PROJ_STEPS):
+        load(step).wait()
+        value = jnp.dot(x_ref[step % PROJ_SLOTS], w_ref[...], preferred_element_type=f32)
+        if step + PROJ_SLOTS < PROJ_STEPS:
+            load(step + PROJ_SLOTS).start()
+        proj_ref[part(step), :] = value
+        scale = lax.rsqrt(jnp.sum(value * value, axis=1, keepdims=True) + epsilon)
+        emb_ref[part(step), :] = (value * scale).astype(bf16)
+        for store in stores(step):
+            store.start()
+    for step in range(PROJ_STEPS):
+        for store in stores(step):
+            store.wait()
 
 
 def project(rows, weight):
     total = rows.shape[0]
-    block = 512
+    vmem = pl.BlockSpec(memory_space=pltpu.VMEM)
+    hbm = pl.BlockSpec(memory_space=pltpu.HBM)
     return pl.pallas_call(
         project_kernel,
-        grid=(total // block,),
-        in_specs=[
-            pl.BlockSpec((block, D_FEAT), lambda i: (i, 0)),
-            pl.BlockSpec((D_FEAT, PROJ), lambda i: (0, 0)),
-        ],
-        out_specs=[
-            pl.BlockSpec((block, PROJ), lambda i: (i, 0)),
-            pl.BlockSpec((block, PROJ), lambda i: (i, 0)),
-        ],
+        in_specs=[hbm, vmem],
+        out_specs=[hbm, hbm],
         out_shape=[
             jax.ShapeDtypeStruct((total, PROJ), f32),
             jax.ShapeDtypeStruct((total, PROJ), bf16),
         ],
-        compiler_params=pltpu.CompilerParams(vmem_limit_bytes=32 * MIB),
+        scratch_shapes=[
+            pltpu.VMEM((PROJ_SLOTS, PROJ_ROWS, D_FEAT), bf16),
+            pltpu.VMEM((total, PROJ), f32),
+            pltpu.VMEM((total, PROJ), bf16),
+            pltpu.SemaphoreType.DMA((PROJ_SLOTS,)),
+            pltpu.SemaphoreType.DMA((PROJ_STEPS,)),
+            pltpu.SemaphoreType.DMA((PROJ_STEPS,)),
+        ],
+        compiler_params=pltpu.CompilerParams(vmem_limit_bytes=58 * MIB),
         cost_estimate=pl.CostEstimate(
             flops=2 * total * D_FEAT * PROJ,
             bytes_accessed=total * (2 * D_FEAT + 6 * PROJ),
@@ -164,7 +201,8 @@
     slot_row = jnp.sum(jnp.where(at, entry_id - ENTRIES, 0), axis=0, keepdims=True) + ENTRIES
     row_of = (query // QBLOCK) * QSTRIDE + (query % QBLOCK) * QTOK
     row_row = jnp.sum(jnp.where(at, row_of, 0), axis=0, keepdims=True)
-    query_row = jnp.sum(jnp.where(at, query * QTOK, 0), axis=0, keepdims=True)
+    out_row = (query // QBLOCK) * RSTRIDE + (query % QBLOCK) * QTOK
+    query_row = jnp.sum(jnp.where(at, out_row, 0), axis=0, keepdims=True)
     start_col = row_to_col(start, 128)[0:P_DEV]
     chunk_page = (
         jnp.sum(
@@ -190,41 +228,57 @@
     return jnp.concatenate(parts, axis=0)
 
 
-def load_page(emb_ref, table_ref, chunk):
-    return emb_ref[pl.ds(pl.multiple_of(table_ref[3, chunk], TOKP), TOKP), :]
-
-
-def forward_kernel(recv_ref, emb_ref, back_ref, table_out, logs_ref, exps_ref, table_ref, logs_of, sem):
+def page_rows(table_ref, chunk):
+    return pl.ds(pl.multiple_of(table_ref[3, chunk], TOKP), TOKP)
+
+
+def chunk_sims(recv_ref, emb_ref, table_ref, chunk):
+    return contract_last(
+        emb_ref[page_rows(table_ref, chunk), :], load_queries(recv_ref, table_ref, chunk)
+    )
+
+
+def chunk_before(chunk, back):
+    return jnp.where(chunk < back, EMPTY_CHUNK, chunk - back)
+
+
+def forward_kernel(
+    recv_ref, emb_hbm, back_ref, table_out, exps_ref, emb_ref, table_ref, logs_of, sims_ref, sems
+):
+    emb_copy = pltpu.make_async_copy(emb_hbm, emb_ref, sems.at[1])
+    emb_copy.start()
     page, query, positive = slot_columns(recv_ref)
     table_out[...] = plan_entries(page, query)
-    copy = pltpu.make_async_copy(table_out, table_ref, sem)
+    copy = pltpu.make_async_copy(table_out, table_ref, sems.at[0])
     copy.start()
+    sims_ref[...] = jnp.zeros(sims_ref.shape, f32)
     copy.wait()
+    emb_copy.wait()
     group = iota((1, 128), 1) // QTOK
 
-    def pair(step, carry):
-        for u in range(2):
-            chunk = 2 * step + u
-            sims = contract_last(
-                load_page(emb_ref, table_ref, chunk), load_queries(recv_ref, table_ref, chunk)
-            )
-            logs = jnp.log2(jnp.sum(jnp.exp2(sims * exp2_factor), axis=0, keepdims=True))
-            logs_ref[pl.ds(chunk, 1), :] = logs
+    def steps(step, carry):
+        for u in range(UNROLL):
+            chunk = UNROLL * step + u
+            sims_ref[u % 2] = chunk_sims(recv_ref, emb_ref, table_ref, chunk)
+            chunk = chunk_before(chunk, 1)
+            expw = jnp.exp2(sims_ref[(u + 1) % 2] * exp2_factor)
+            logs = jnp.log2(jnp.sum(expw, axis=0, keepdims=True))
             for j in range(CHUNK):
                 tile = logs[:, (j // 4) * 128 : (j // 4) * 128 + 128]
                 slot = table_ref[0, chunk * CHUNK + j]
                 logs_of[pl.ds(slot, 1), :] = jnp.where(group == j % 4, tile, 0.0)
         return carry
 
-    lax.fori_loop(0, (table_ref[3, 128] + 1) // 2, pair, 0)
+    lax.fori_loop(0, (table_ref[3, 128] + 1 + UNROLL - 1) // UNROLL, steps, 0)
+    valid = page >= 0
     scores = log2_factor * jnp.sum(logs_of[0:ENTRIES, :], axis=1, keepdims=True)
-    valid = page >= 0
+    scores = jnp.where(valid, scores, 0.0)
     exps = jnp.where(valid, jnp.exp(scores), 0.0)
     exps_ref[...] = jnp.broadcast_to(exps, (ENTRIES, 128))
     lane = iota((ENTRIES, 128), 1)
     sums = jnp.sum(jnp.where(query == lane, exps, 0.0), axis=0, keepdims=True)
     slot = iota((ENTRIES, 128), 0) % SLOTS
-    spread = jnp.where((lane == slot) & valid, scores, 0.0).reshape(OWNERS, SLOTS, 128)
+    spread = jnp.where(lane == slot, scores, 0.0).reshape(OWNERS, SLOTS, 128)
     spread = jnp.sum(spread, axis=1, keepdims=True)
     which = iota((OWNERS, SLOTS, 128), 1)
     back_ref[...] = jnp.where(
@@ -233,40 +287,47 @@
 
 
 def forward(recv, emb):
+    vmem = pl.BlockSpec(memory_space=pltpu.VMEM)
     return pl.pallas_call(
         forward_kernel,
+        in_specs=[vmem, pl.BlockSpec(memory_space=pltpu.HBM)],
+        out_specs=[vmem, vmem, vmem],
         out_shape=[
             jax.ShapeDtypeStruct((OWNERS, SLOTS, 128), f32),
             jax.ShapeDtypeStruct((8, POSITIONS), i32),
-            jax.ShapeDtypeStruct((MAX_CHUNKS, LANES), f32),
             jax.ShapeDtypeStruct((ENTRIES, 128), f32),
         ],
         scratch_shapes=[
+            pltpu.VMEM((P_DEV * TOKP, PROJ), bf16),
             pltpu.SMEM((8, POSITIONS), i32),
             pltpu.VMEM((ENTRIES + 8, 128), f32),
-            pltpu.SemaphoreType.DMA,
+            pltpu.VMEM((2, TOKP, LANES), f32),
+            pltpu.SemaphoreType.DMA((2,)),
         ],
-        compiler_params=pltpu.CompilerParams(vmem_limit_bytes=32 * MIB),
+        compiler_params=pltpu.CompilerParams(vmem_limit_bytes=58 * MIB),
         name="forward",
     )(recv, emb)
 
 
-FEAT_PAGES = 4
-FEAT_ROWS = FEAT_PAGES * TOKP
-FEAT_STEPS = P_DEV // FEAT_PAGES
+FEAT_STEPS = 10
+FEAT_SLOTS = 6
+FEAT_ROWS = P_DEV * TOKP // FEAT_STEPS
 
 
 def backward_kernel(
-    table_ref, recv_ref, emb_ref, logs_ref, exps_ref, sums_ref, proj_hbm, feat_hbm,
-    query_out, grad_out, weight_of, page_acc, query_acc, proj_ref, feat_ref, sems,
+    table_ref, recv_ref, exps_ref, sums_ref, emb_hbm, proj_hbm, feat_hbm, out_ref,
+    weight_of, page_acc, query_acc, emb_ref, proj_ref, grad_ref, feat_ref, sims_ref, grads_ref, sems,
 ):
     def feature_copy(step):
         part = pl.ds(step * FEAT_ROWS, FEAT_ROWS)
-        return pltpu.make_async_copy(feat_hbm.at[part], feat_ref.at[part], sems.at[step])
-
-    proj_copy = pltpu.make_async_copy(proj_hbm, proj_ref, sems.at[FEAT_STEPS])
+        slot = step % FEAT_SLOTS
+        return pltpu.make_async_copy(feat_hbm.at[part], feat_ref.at[slot], sems.at[slot])
+
+    emb_copy = pltpu.make_async_copy(emb_hbm, emb_ref, sems.at[FEAT_SLOTS])
+    emb_copy.start()
+    proj_copy = pltpu.make_async_copy(proj_hbm, proj_ref, sems.at[FEAT_SLOTS + 1])
     proj_copy.start()
-    for step in range(FEAT_STEPS):
+    for step in range(FEAT_SLOTS):
         feature_copy(step).start()
 
     page, query, positive = slot_columns(recv_ref)
@@ -281,81 +342,144 @@
     weight_of[ENTRIES : ENTRIES + 8, :] = jnp.zeros((8, 128), f32)
     page_acc[...] = jnp.zeros(page_acc.shape, f32)
     query_acc[...] = jnp.zeros(query_acc.shape, f32)
+    sims_ref[...] = jnp.zeros(sims_ref.shape, f32)
+    grads_ref[...] = jnp.zeros(grads_ref.shape, bf16)
+    emb_copy.wait()
     group = iota((1, 128), 1) // QTOK
 
-    def pair(step, carry):
-        results = []
-        for u in range(2):
-            chunk = 2 * step + u
-            tokens = load_page(emb_ref, table_ref, chunk)
-            queries = load_queries(recv_ref, table_ref, chunk)
-            weights = []
-            for half in range(CHUNK // 4):
-                tile = jnp.zeros((1, 128), f32)
-                for j in range(4):
-                    slot = table_ref[0, chunk * CHUNK + half * 4 + j]
-                    tile = jnp.where(group == j, weight_of[pl.ds(slot, 1), :], tile)
-                weights.append(tile)
-            weights = jnp.concatenate(weights, axis=1)
-            sims = contract_last(tokens, queries)
-            share = jnp.exp2(sims * exp2_factor - logs_ref[pl.ds(chunk, 1), :])
-            sim_grad = (share * weights).astype(bf16)
-            page_part = jnp.dot(sim_grad, queries, preferred_element_type=f32)
-            query_part = contract_first(sim_grad, tokens)
-            results.append((chunk, page_part, query_part))
-        for chunk, page_part, query_part in results:
-            rows = pl.ds(pl.multiple_of(table_ref[3, chunk], TOKP), TOKP)
+    def chunk_weights(chunk):
+        tiles = []
+        for half in range(CHUNK // 4):
+            tile = jnp.zeros((1, 128), f32)
+            for j in range(4):
+                slot = table_ref[0, chunk * CHUNK + half * 4 + j]
+                tile = jnp.where(group == j, weight_of[pl.ds(slot, 1), :], tile)
+            tiles.append(tile)
+        return jnp.concatenate(tiles, axis=1)
+
+    def steps(step, carry):
+        for u in range(UNROLL):
+            chunk = UNROLL * step + u
+            now, last = u % 2, (u + 1) % 2
+            sims_ref[now] = chunk_sims(recv_ref, emb_ref, table_ref, chunk)
+
+            middle = chunk_before(chunk, 1)
+            expw = jnp.exp2(sims_ref[last] * exp2_factor)
+            ratio = chunk_weights(middle) / jnp.sum(expw, axis=0, keepdims=True)
+            grads_ref[last] = (expw * ratio).astype(bf16)
+
+            oldest = chunk_before(chunk, 2)
+            rows = page_rows(table_ref, oldest)
+            sim_grad = grads_ref[now]
+            page_part = jnp.dot(
+                sim_grad, load_queries(recv_ref, table_ref, oldest), preferred_element_type=f32
+            )
+            query_part = contract_first(sim_grad, emb_ref[rows, :])
             page_acc[rows, :] += page_part
             for j in range(CHUNK):
-                at = pl.ds(pl.multiple_of(table_ref[2, chunk * CHUNK + j], QTOK), QTOK)
+                at = pl.ds(pl.multiple_of(table_ref[2, oldest * CHUNK + j], QTOK), QTOK)
                 query_acc[at, :] += query_part[j * QTOK : (j + 1) * QTOK]
         return carry
 
-    lax.fori_loop(0, (table_ref[3, 128] + 1) // 2, pair, 0)
-    query_out[...] = query_acc[...].astype(query_out.dtype)
+    lax.fori_loop(0, (table_ref[3, 128] + 2 + UNROLL - 1) // UNROLL, steps, 0)
+    out_ref[:, 0:QROWS, :] = query_acc[...].astype(bf16).reshape(OWNERS, QROWS, PROJ)
     proj_copy.wait()
-    grad_out[...] = jnp.zeros(grad_out.shape, f32)
-
-    def feature_step(step, carry):
-        part = pl.ds(pl.multiple_of(step * FEAT_ROWS, FEAT_ROWS), FEAT_ROWS)
+
+    def token_grads(step, carry):
+        part = pl.ds(pl.multiple_of(step * 512, 512), 512)
         value = proj_ref[part, :]
         upstream = page_acc[part, :]
         scale = lax.rsqrt(jnp.sum(value * value, axis=1, keepdims=True) + epsilon)
         inner = jnp.sum(value * upstream, axis=1, keepdims=True)
-        grad = (upstream * scale - value * (scale * scale * scale * inner)).astype(bf16)
+        grad_ref[part, :] = (
+            upstream * scale - value * (scale * scale * scale * inner)
+        ).astype(bf16)
+        return carry
+
+    lax.fori_loop(0, P_DEV * TOKP // 512, token_grads, 0)
+    grad = jnp.zeros((PROJ, D_FEAT), f32)
+    for step in range(FEAT_STEPS):
+        part = pl.ds(step * FEAT_ROWS, FEAT_ROWS)
         feature_copy(step).wait()
-        grad_out[...] += contract_first(feat_ref[part, :], grad)
-        return carry
-
-    lax.fori_loop(0, FEAT_STEPS, feature_step, 0)
-
-
-def backward(table, recv, emb, logs, exps, sums, proj, rows):
+        grad += contract_first(grad_ref[part, :], feat_ref[step % FEAT_SLOTS])
+        if step + FEAT_SLOTS < FEAT_STEPS:
+            feature_copy(step + FEAT_SLOTS).start()
+    grad = grad.T
+    for owner in range(OWNERS):
+        rows = grad[owner * GRAD_ROWS : (owner + 1) * GRAD_ROWS]
+        rows = jnp.concatenate([rows, jnp.zeros((GRAD_PAD - GRAD_ROWS, PROJ), f32)], axis=0)
+        out_ref[owner, QROWS : QROWS + GRAD_PAD, :] = rows.astype(bf16)
+
+
+def backward(table, recv, exps, sums, emb, proj, rows):
     vmem = pl.BlockSpec(memory_space=pltpu.VMEM)
-    hbm = pl.BlockSpec(memory_space=pl.ANY)
+    hbm = pl.BlockSpec(memory_space=pltpu.HBM)
     return pl.pallas_call(
         backward_kernel,
-        in_specs=[pl.BlockSpec(memory_space=pltpu.SMEM), vmem, vmem, vmem, vmem, vmem, hbm, hbm],
-        out_specs=[vmem, vmem],
-        out_shape=[
-            jax.ShapeDtypeStruct((OWNERS * QROWS, PROJ), bf16),
-            jax.ShapeDtypeStruct((D_FEAT, PROJ), f32),
-        ],
+        in_specs=[pl.BlockSpec(memory_space=pltpu.SMEM), vmem, vmem, vmem, hbm, hbm, hbm],
+        out_specs=vmem,
+        out_shape=jax.ShapeDtypeStruct((OWNERS, QROWS + GRAD_PAD, PROJ), bf16),
         scratch_shapes=[
             pltpu.VMEM((ENTRIES + 8, 128), f32),
             pltpu.VMEM((P_DEV * TOKP, PROJ), f32),
             pltpu.VMEM((OWNERS * QROWS, PROJ), f32),
+            pltpu.VMEM((P_DEV * TOKP, PROJ), bf16),
             pltpu.VMEM((P_DEV * TOKP, PROJ), f32),
-            pltpu.VMEM((P_DEV * TOKP, D_FEAT), bf16),
-            pltpu.SemaphoreType.DMA((FEAT_STEPS + 1,)),
+            pltpu.VMEM((P_DEV * TOKP, PROJ), bf16),
+            pltpu.VMEM((FEAT_SLOTS, FEAT_ROWS, D_FEAT), bf16),
+            pltpu.VMEM((2, TOKP, LANES), f32),
+            pltpu.VMEM((2, TOKP, LANES), bf16),
+            pltpu.SemaphoreType.DMA((FEAT_SLOTS + 2,)),
         ],
-        compiler_params=pltpu.CompilerParams(vmem_limit_bytes=60 * MIB),
+        compiler_params=pltpu.CompilerParams(vmem_limit_bytes=58 * MIB),
         name="backward",
-    )(table, recv, emb, logs, exps, sums, proj, rows)
+    )(table, recv, exps, sums, emb, proj, rows)
+
+
+def share_kernel(parts_ref, out_ref):
+    out_ref[...] = jnp.sum(parts_ref[:, QROWS : QROWS + GRAD_PAD, :].astype(f32), axis=0)
+
+
+def own_share(parts):
+    return pl.pallas_call(
+        share_kernel,
+        out_shape=jax.ShapeDtypeStruct((GRAD_PAD, PROJ), f32),
+        compiler_params=SMALL,
+        name="own_share",
+    )(parts)
+
+
+def spread_kernel(a_ref, b_ref, c_ref, d_ref, out_ref):
+    total = (a_ref[...] + b_ref[...]) + (c_ref[...] + d_ref[...])
+    out_ref[...] = jnp.broadcast_to(total.astype(bf16)[None], out_ref.shape)
+
+
+def spread_share(shares):
+    return pl.pallas_call(
+        spread_kernel,
+        out_shape=jax.ShapeDtypeStruct((OWNERS, GRAD_PAD, PROJ), bf16),
+        compiler_params=SMALL,
+        name="spread_share",
+    )(*shares)
+
+
+def collect_kernel(parts_ref, out_ref):
+    for owner in range(OWNERS):
+        rows = parts_ref[owner].astype(f32)[0:GRAD_ROWS]
+        out_ref[owner * GRAD_ROWS : (owner + 1) * GRAD_ROWS, :] = rows
+
+
+def collect(parts):
+    return pl.pallas_call(
+        collect_kernel,
+        out_shape=jax.ShapeDtypeStruct((D_FEAT, PROJ), f32),
+        compiler_params=SMALL,
+        name="collect",
+    )(parts)
 
 
 def query_kernel(parts_ref, q_ref, out_ref):
-    upstream = jnp.sum(parts_ref[...].astype(f32), axis=0)
+    upstream = jnp.sum(parts_ref[:, 0:QROWS, :].astype(f32), axis=0)
     wide = q_ref[...].reshape(QROWS, PROJ).astype(f32)
     scale = lax.rsqrt(jnp.sum(wide * wide, axis=1, keepdims=True) + epsilon)
     inner = jnp.sum(wide * upstream, axis=1, keepdims=True)
@@ -368,7 +492,7 @@
     return pl.pallas_call(
         query_kernel,
         out_shape=jax.ShapeDtypeStruct(queries.shape, f32),
-        compiler_params=pltpu.CompilerParams(vmem_limit_bytes=32 * MIB),
+        compiler_params=SMALL,
         name="query_grads",
     )(parts, queries)
 
@@ -387,21 +511,20 @@
 
 
 def per_device(features, queries, proj_weight, page_ids):
-    everyone = ("pages", "rep")
-    devices = lax.axis_size(everyone)
     rows = features.reshape(P_DEV * TOKP, D_FEAT)
     recv = exchange(send_queries(page_ids, queries), "pages").reshape(OWNERS * QSTRIDE, PROJ)
     proj, emb = project(rows, proj_weight)
-    back, table, logs, exps = forward(recv, emb)
+    back, table, exps = forward(recv, emb)
     sums = exchange(back, "pages")
-    query_parts, local_term = backward(table, recv, emb, logs, exps, sums, proj, rows)
-    parts = exchange(query_parts.reshape(OWNERS, QROWS, PROJ), "pages")
+    parts = exchange(backward(table, recv, exps, sums, emb, proj, rows), "pages")
+    share = own_share(parts)
+    replicas = lax.axis_size("rep")
+    shares = [share] + [
+        lax.ppermute(share, "rep", [(i, i ^ k) for i in range(replicas)]) for k in (1, 2, 3)
+    ]
+    grad_proj = collect(exchange(spread_share(shares), "pages"))
     grad_query = query_grads(parts, queries)
     scores = listed_scores(sums, page_ids)
-    shares = exchange(local_term.astype(bf16).reshape(devices, D_FEAT // devices, PROJ), everyone)
-    share = jnp.sum(shares.astype(f32), axis=0).astype(bf16)
-    whole = exchange(jnp.broadcast_to(share[None], shares.shape), everyone)
-    grad_proj = whole.reshape(D_FEAT, PROJ).astype(f32)
     return (scores, grad_query, grad_proj)
 
 

time: 154 us -> 128 us (0.83)
  blocking collectives: 45.3 us -> 15.3 us
  starting transfers between devices: 17 us -> 27.5 us
  local copies, waits for them, and re-layouts: 10.4 us -> 4.28 us
  Pallas kernels: 50.8 us -> 45.4 us
  waiting for transfers between devices: 27.7 us -> 32.7 us
    all_to_all x2 -> x1, blocking collectives: 45.3 us -> 15.3 us  [exchange(): return lax.all_to_all(values, axes, split_axis=0, concat_axis=0, tiled=True)]
    all_to_all x3, starting transfers between devices: 17 us -> 23 us  [exchange(): return lax.all_to_all(values, axes, split_axis=0, concat_axis=0, tiled=True)]
    ppermute x0 -> x3, starting transfers between devices: none -> 4.51 us  [per_device(): lax.ppermute(share, 'rep', [(i, i ^ k) for i in range(replicas)])]
    pallas_call x1, Pallas kernels: 22.6 us -> 18.3 us  [backward(): pl.pallas_call(backward_kernel, in_specs=[pl.BlockSpec(memory_space=pltpu...]
    unnamed x20 -> x10, local copies, waits for them, and re-layouts: 6.61 us -> 2.44 us
    ppermute x0 -> x3, waiting for transfers between devices: none -> 4.01 us  [per_device(): lax.ppermute(share, 'rep', [(i, i ^ k) for i in range(replicas)])]
    pallas_call x2 -> x5, Pallas kernels: 24.9 us -> 24.6 us  [the longest x1 16.8 us: project(): pl.pallas_call(project_kernel, in_specs=[hbm, vmem], out_specs=[hbm, hbm]...]
  transfers between devices with their start and end apart: 3 -> 6, of which waited for: 2 -> 5; matrix products, arithmetic and copies ran while one was open for 2% -> 2% of each run, Pallas kernels for 13% -> 14%
where the time goes in v2:
time: 128 us; the launch traced here: 127 us
  Pallas kernels  45.4 us (35%)
  waiting for transfers between devices  32.7 us (26%)
  starting transfers between devices  27.5 us (21%)
  blocking collectives  15.3 us (12%)
  local copies, waits for them, and re-layouts  4.28 us (3%)
    all_to_all x3, waiting for transfers between devices, exchange(): return lax.all_to_all(values, axes, split_axis=0, concat_axis=0, tiled=True)  28.7 us
    all_to_all x3, starting transfers between devices, exchange(): return lax.all_to_all(values, axes, split_axis=0, concat_axis=0, tiled=True)  23 us
    pallas_call x1, Pallas kernels, backward(): pl.pallas_call(backward_kernel, in_specs=[pl.BlockSpec(memory_space=pltpu...  18.3 us
    pallas_call x1, Pallas kernels, project(): pl.pallas_call(project_kernel, in_specs=[hbm, vmem], out_specs=[hbm, hbm]...  16.8 us
    all_to_all x1, blocking collectives, exchange(): return lax.all_to_all(values, axes, split_axis=0, concat_axis=0, tiled=True)  15.3 us
    pallas_call x1, Pallas kernels, forward(): pl.pallas_call(forward_kernel, in_specs=[vmem, pl.BlockSpec(memory_space=...  6.08 us
    ppermute x3, starting transfers between devices, per_device(): lax.ppermute(share, 'rep', [(i, i ^ k) for i in range(replicas)])  4.51 us
    ppermute x3, waiting for transfers between devices, per_device(): lax.ppermute(share, 'rep', [(i, i ^ k) for i in range(replicas)])  4.01 us
  transfers between devices with their start and end apart: 6, of which 5 were waited for; matrix products, arithmetic and copies ran while one was open for 2% of the time, Pallas kernels for 14%

profile of v2, /device:TPU:1, one launch (start us, length us, event | category | flops | bytes accessed | tf_op | source)
XLA Modules:
  0.0 126.5 jit_solution(18132377900023539287)
XLA Ops:
  0.6 0.0 copy-start
  0.6 0.7 copy-done
  1.4 0.0 copy-start.2
  1.4 0.7 copy-done.2
  2.1 1.6 %send_queries.1 = bf16[32,144,128]{2,1,0:T(8,128)(2,1)} custom-call(s32[4,16]{1,0:T(4,128)S(1)} %copy-done.2, bf16[4,32,128]{2,1,0:T(8,128)(2,1)S(1)} %copy-done), custom_call_target="tpu_custom_call" | custom-call | tf_op jit(solution)/shard_map/send_queries/pallas_call | solution.py:98
  3.7 8.6 %all-to-all-start = ((bf16[32,144,128]{2,1,0:T(8,128)(2,1)}), bf16[32,144,128]{2,1,0:T(8,128)(2,1)S(1)}, u32[]{:S(2)}, u32[]{:S(2)}) async-start(bf16[32,144,128]{2,1,0:T(8,128)(2,1)} %send_queries.1), calls=%async_computation | async-start | bytes 2359296 | tf_op jit(solution)/shard_map/all_to_all | solution.py:510
  12.3 16.8 %project.1 = (f32[10240,128]{1,0:T(8,128)}, bf16[10240,128]{1,0:T(8,128)(2,1)}) custom-call(bf16[10240,1152]{1,0:T(8,128)(2,1)} %bitcast.3, bf16[1152,128]{1,0:T(8,128)(2,1)} %w_ref.1), custom_call_target="tpu_custom_call" | custom-call | flops 3019898880 | bytes 31457280 | tf_op jit(solution)/shard_map/project/pallas_call | solution.py:146
  29.1 0.9 all-to-all-done
  30.0 0.0 copy-start.4
  30.0 1.0 copy-done.4
  31.0 6.1 %forward.1 = (f32[32,8,128]{2,1,0:T(8,128)}, s32[8,640]{1,0:T(8,128)}, f32[256,128]{1,0:T(8,128)}) custom-call(bf16[4608,128]{1,0:T(8,128)(2,1)} %bitcast.5, bf16[10240,128]{1,0:T(8,128)(2,1)} %get-tuple-element.8.emb_hbm), custom_call_target="tpu_custom_call" | custom-call | tf_op jit(solution)/shard_map/forward/pallas_call | solution.py:291
  37.1 15.3 %all_to_all.20.sums_ref = f32[32,8,128]{2,1,0:T(8,128)} all-to-all(f32[32,8,128]{2,1,0:T(8,128)} %get-tuple-element.9), channel_id=1, replica_groups=mesh['pages'=32,'rep'=4] {'pages'}, dimensions={0} | all-to-all | bytes 262144 | tf_op jit(solution)/shard_map/all_to_all | solution.py:510
  52.4 18.3 %backward.1 = bf16[32,176,128]{2,1,0:T(8,128)(2,1)} custom-call(s32[8,640]{1,0:T(8,128)} %get-tuple-element.10.table_ref, bf16[4608,128]{1,0:T(8,128)(2,1)} %bitcast.6, f32[256,128]{1,0:T(8,128)} %get-tuple-element.11.exps_ref, f32[32,8,128]{2,1,0:T(8,128)} %all_to_all.20.sums_ref, bf16[10240,128]{1,0:T(8,128)(2,1)} %get-tuple-element.8.emb_hbm, ...), custom_call_target="tpu_custom_call" | custom-call | tf_op jit(solution)/shard_map/backward/pallas_call | solution.py:417
  70.8 0.0 copy-start.3
  70.8 7.5 %all-to-all-start.2 = ((bf16[32,176,128]{2,1,0:T(8,128)(2,1)}), bf16[32,176,128]{2,1,0:T(8,128)(2,1)S(1)}, u32[]{:S(2)}, u32[]{:S(2)}) async-start(bf16[32,176,128]{2,1,0:T(8,128)(2,1)} %backward.1), calls=%async_computation.2 | async-start | bytes 2883584 | tf_op jit(solution)/shard_map/all_to_all | solution.py:510
  78.3 0.0 copy-done.3
  78.3 0.1 div.14
  78.4 0.1 and.25
  78.5 0.1 broadcast_compare_fusion
  78.6 0.1 reduce_window_sum.11
  78.7 0.0 copy-start.1
  78.7 20.2 %all-to-all-done.2.parts_ref = bf16[32,176,128]{2,1,0:T(8,128)(2,1)S(1)} async-done(((bf16[32,176,128]{2,1,0:T(8,128)(2,1)}), bf16[32,176,128]{2,1,0:T(8,128)(2,1)S(1)}, u32[]{:S(2)}, u32[]{:S(2)}) %all-to-all-start.2) | async-done | bytes 1441824 | tf_op jit(solution)/shard_map/all_to_all | solution.py:510
  98.9 0.1 own_share.1.a_ref
  99.0 1.7 %collective-permute-start = (f32[48,128]{1,0:T(8,128)S(1)}, f32[48,128]{1,0:T(8,128)S(1)}, u32[]{:S(2)}, u32[]{:S(2)}) collective-permute-start(f32[48,128]{1,0:T(8,128)S(1)} %own_share.1.a_ref), channel_id=1, source_target_pairs={{0,1},{1,0},{2,3},{3,2},{4,5},{5,4},{6,7},{7,6},{8,9},{9,8},{10,11... | collective-permute-start | bytes 73736 | tf_op jit(solution)/shard_map/ppermute | solution.py:523
  100.7 2.8 %collective-permute-start.1 = (f32[48,128]{1,0:T(8,128)S(1)}, f32[48,128]{1,0:T(8,128)S(1)}, u32[]{:S(2)}, u32[]{:S(2)}) collective-permute-start(f32[48,128]{1,0:T(8,128)S(1)} %own_share.1.a_ref), channel_id=1, source_target_pairs={{0,2},{1,3},{2,0},{3,1},{4,6},{5,7},{6,4},{7,5},{8,10},{9,11},{10,... | collective-permute-start | bytes 73736 | tf_op jit(solution)/shard_map/ppermute | solution.py:523
  103.5 0.0 collective-permute-start.2
  103.5 0.2 select_reduce_fusion.1
  103.7 0.0 collective-permute-done.b_ref
  103.7 1.3 %collective-permute-done.1.c_ref = f32[48,128]{1,0:T(8,128)S(1)} collective-permute-done((f32[48,128]{1,0:T(8,128)S(1)}, f32[48,128]{1,0:T(8,128)S(1)}, u32[]{:S(2)}, u32[]{:S(2)}) %collective-permute-start.1) | collective-permute-done | bytes 24608 | tf_op jit(solution)/shard_map/ppermute | solution.py:523
  105.0 2.7 %collective-permute-done.2.d_ref = f32[48,128]{1,0:T(8,128)S(1)} collective-permute-done((f32[48,128]{1,0:T(8,128)S(1)}, f32[48,128]{1,0:T(8,128)S(1)}, u32[]{:S(2)}, u32[]{:S(2)}) %collective-permute-start.2) | collective-permute-done | bytes 24608 | tf_op jit(solution)/shard_map/ppermute | solution.py:523
  107.7 0.8 spread_share.1
  108.5 6.9 %all-to-all-start.3 = ((bf16[32,48,128]{2,1,0:T(8,128)(2,1)}), bf16[32,48,128]{2,1,0:T(8,128)(2,1)S(1)}, u32[]{:S(2)}, u32[]{:S(2)}) async-start(bf16[32,48,128]{2,1,0:T(8,128)(2,1)} %spread_share.1), calls=%async_computation.3 | async-start | bytes 786432 | tf_op jit(solution)/shard_map/all_to_all | solution.py:510
  115.4 0.1 copy.7
  115.5 0.9 slice.4
  116.4 0.1 select_reduce_fusion
  116.5 0.7 reshape.89
  117.2 0.0 copy-done.1
  117.2 0.9 query_grads.1
  118.1 7.6 %all-to-all-done.3.parts_ref = bf16[32,48,128]{2,1,0:T(8,128)(2,1)S(1)} async-done(((bf16[32,48,128]{2,1,0:T(8,128)(2,1)}), bf16[32,48,128]{2,1,0:T(8,128)(2,1)S(1)}, u32[]{:S(2)}, u32[]{:S(2)}) %all-to-all-start.3) | async-done | bytes 393248 | tf_op jit(solution)/shard_map/all_to_all | solution.py:510
  125.7 0.9 collect.1
  (5 shorter events, 0.0 us)
Async XLA Ops:
  0.6 0.8 copy-start
  1.4 0.7 copy-start.2
  3.7 26.3 %all-to-all-start = ((bf16[32,144,128]{2,1,0:T(8,128)(2,1)}), bf16[32,144,128]{2,1,0:T(8,128)(2,1)S(1)}, u32[]{:S(2)}, u32[]{:S(2)}) async-start(bf16[32,144,128]{2,1,0:T(8,128)(2,1)} %send_queries.1), calls=%async_computation | async-start | bytes 2359296 | tf_op jit(solution)/shard_map/all_to_all | solution.py:510
  30.0 1.0 copy-start.4
  70.8 7.6 %copy-start.3 = (s32[4,16]{1,0:T(4,128)S(1)}, s32[4,16]{1,0:T(4,128)}, u32[]{:S(2)}) copy-start(s32[4,16]{1,0:T(4,128)} %ids_ref.1) | copy-start | bytes 772
  70.8 28.2 %all-to-all-start.2 = ((bf16[32,176,128]{2,1,0:T(8,128)(2,1)}), bf16[32,176,128]{2,1,0:T(8,128)(2,1)S(1)}, u32[]{:S(2)}, u32[]{:S(2)}) async-start(bf16[32,176,128]{2,1,0:T(8,128)(2,1)} %backward.1), calls=%async_computation.2 | async-start | bytes 2883584 | tf_op jit(solution)/shard_map/all_to_all | solution.py:510
  78.7 38.5 %copy-start.1 = (bf16[4,32,128]{2,1,0:T(8,128)(2,1)S(1)}, bf16[4,32,128]{2,1,0:T(8,128)(2,1)}, u32[]{:S(2)}) copy-start(bf16[4,32,128]{2,1,0:T(8,128)(2,1)} %q_ref.3) | copy-start | bytes 98308
  99.0 4.7 %collective-permute-start = (f32[48,128]{1,0:T(8,128)S(1)}, f32[48,128]{1,0:T(8,128)S(1)}, u32[]{:S(2)}, u32[]{:S(2)}) collective-permute-start(f32[48,128]{1,0:T(8,128)S(1)} %own_share.1.a_ref), channel_id=1, source_target_pairs={{0,1},{1,0},{2,3},{3,2},{4,5},{5,4},{6,7},{7,6},{8,9},{9,8},{10,11... | collective-permute-start | bytes 73736 | tf_op jit(solution)/shard_map/ppermute | solution.py:523
  100.7 4.3 %collective-permute-start.1 = (f32[48,128]{1,0:T(8,128)S(1)}, f32[48,128]{1,0:T(8,128)S(1)}, u32[]{:S(2)}, u32[]{:S(2)}) collective-permute-start(f32[48,128]{1,0:T(8,128)S(1)} %own_share.1.a_ref), channel_id=1, source_target_pairs={{0,2},{1,3},{2,0},{3,1},{4,6},{5,7},{6,4},{7,5},{8,10},{9,11},{10,... | collective-permute-start | bytes 73736 | tf_op jit(solution)/shard_map/ppermute | solution.py:523
  103.5 4.2 %collective-permute-start.2 = (f32[48,128]{1,0:T(8,128)S(1)}, f32[48,128]{1,0:T(8,128)S(1)}, u32[]{:S(2)}, u32[]{:S(2)}) collective-permute-start(f32[48,128]{1,0:T(8,128)S(1)} %own_share.1.a_ref), channel_id=1, source_target_pairs={{0,3},{1,2},{2,1},{3,0},{4,7},{5,6},{6,5},{7,4},{8,11},{9,10},{10,... | collective-permute-start | bytes 73736 | tf_op jit(solution)/shard_map/ppermute | solution.py:523
  108.5 17.2 %all-to-all-start.3 = ((bf16[32,48,128]{2,1,0:T(8,128)(2,1)}), bf16[32,48,128]{2,1,0:T(8,128)(2,1)S(1)}, u32[]{:S(2)}, u32[]{:S(2)}) async-start(bf16[32,48,128]{2,1,0:T(8,128)(2,1)} %spread_share.1), calls=%async_computation.3 | async-start | bytes 786432 | tf_op jit(solution)/shard_map/all_to_all | solution.py:510

commit v3 on v2

--- a/solution.py
+++ b/solution.py
@@ -33,10 +33,10 @@
 LANES = CHUNK * QTOK
 GRAD_ROWS = D_FEAT // OWNERS
 GRAD_PAD = 48
-RSTRIDE = QROWS
+CHIPS = OWNERS // 2
 POSITIONS = 640
 EMPTY_CHUNK = POSITIONS // CHUNK - 1
-UNROLL = 4
+UNROLL = 6
 MIB = 1 << 20
 SMALL = pltpu.CompilerParams(vmem_limit_bytes=8 * MIB)
 
@@ -67,7 +67,7 @@
     wide = q_ref[...].reshape(QROWS, PROJ).astype(f32)
     scale = lax.rsqrt(jnp.sum(wide * wide, axis=1, keepdims=True) + epsilon)
     emb = (wide * scale).astype(bf16)
-    out_ref[:, 0:QROWS, :] = jnp.broadcast_to(emb[None], (OWNERS, QROWS, PROJ))
+    out_ref[:, 0:QROWS, :] = jnp.broadcast_to(emb[None], (CHIPS, QROWS, PROJ))
     ids = ids_ref[...].astype(f32)
     owner = jnp.floor((ids + 0.5) * (1.0 / P_DEV))
     local = ids - owner * P_DEV
@@ -82,56 +82,72 @@
         hit * jnp.dot(before, hit, preferred_element_type=f32), axis=1, keepdims=True
     ).astype(i32)
     code = (entry // LISTED) * 2 + (entry % LISTED == 0).astype(i32)
+    base = rank + 2 * SLOTS * (owner_col.astype(i32) % 2)
     value = jnp.where(
-        rank == lane,
+        base == lane,
         local_col + 1.0,
-        jnp.where(rank + SLOTS == lane, code.astype(f32), 0.0),
-    )
-    value = jnp.where(lane < 2 * SLOTS, value, 0.0)
-    meta = contract_first(hit, value)[0:OWNERS]
+        jnp.where(base + SLOTS == lane, code.astype(f32), 0.0),
+    )
+    on_chip = (owner_col.astype(i32) // 2 == lane).astype(f32)
+    meta = contract_first(on_chip, value)[0:CHIPS]
     out_ref[:, QROWS:QSTRIDE, :] = jnp.broadcast_to(
-        meta[:, None, :], (OWNERS, META, PROJ)
+        meta[:, None, :], (CHIPS, META, PROJ)
     ).astype(bf16)
 
 
 def send_queries(page_ids, queries):
     return pl.pallas_call(
         send_kernel,
-        out_shape=jax.ShapeDtypeStruct((OWNERS, QSTRIDE, PROJ), bf16),
-        compiler_params=SMALL,
+        out_shape=jax.ShapeDtypeStruct((CHIPS, QSTRIDE, PROJ), bf16),
+        compiler_params=pltpu.CompilerParams(vmem_limit_bytes=58 * MIB),
         name="send_queries",
     )(page_ids, queries)
 
 
-PROJ_ROWS = 1024
-PROJ_SLOTS = 4
+PROJ_ROWS = 2048
+PROJ_SUB = 512
 PROJ_STEPS = P_DEV * TOKP // PROJ_ROWS
 
 
-def project_kernel(x_hbm, w_ref, proj_hbm, emb_hbm, x_ref, proj_ref, emb_ref, sems, proj_sems, emb_sems):
+def project_kernel(
+    x_hbm, w_ref, emb_hbm, rest_hbm, scale_out, x_ref, value_ref, emb_ref, rest_ref, sems, emb_sems, rest_sems
+):
     def part(step):
         return pl.ds(step * PROJ_ROWS, PROJ_ROWS)
 
     def load(step):
-        slot = step % PROJ_SLOTS
-        return pltpu.make_async_copy(x_hbm.at[part(step)], x_ref.at[slot], sems.at[slot])
+        return pltpu.make_async_copy(x_hbm.at[part(step)], x_ref.at[part(step)], sems.at[step])
 
     def stores(step):
         return (
-            pltpu.make_async_copy(proj_ref.at[part(step)], proj_hbm.at[part(step)], proj_sems.at[step]),
             pltpu.make_async_copy(emb_ref.at[part(step)], emb_hbm.at[part(step)], emb_sems.at[step]),
+            pltpu.make_async_copy(rest_ref.at[part(step)], rest_hbm.at[part(step)], rest_sems.at[step]),
         )
 
-    for step in range(PROJ_SLOTS):
+    def normalize(at):
+        rows = pl.ds(at, PROJ_SUB)
+        value = value_ref[rows, :]
+        scale = lax.rsqrt(jnp.sum(value * value, axis=1, keepdims=True) + epsilon)
+        unit = value * scale
+        emb = unit.astype(bf16)
+        emb_ref[rows, :] = emb
+        rest_ref[rows, :] = (unit - emb.astype(f32)).astype(bf16)
+        for block in range(PROJ_SUB // 128):
+            row = at // 128 + block
+            scale_out[row : row + 1, :] = col_to_row(scale[block * 128 : block * 128 + 128], 128)
+
+    for step in range(PROJ_STEPS):
         load(step).start()
     for step in range(PROJ_STEPS):
         load(step).wait()
-        value = jnp.dot(x_ref[step % PROJ_SLOTS], w_ref[...], preferred_element_type=f32)
-        if step + PROJ_SLOTS < PROJ_STEPS:
-            load(step + PROJ_SLOTS).start()
-        proj_ref[part(step), :] = value
-        scale = lax.rsqrt(jnp.sum(value * value, axis=1, keepdims=True) + epsilon)
-        emb_ref[part(step), :] = (value * scale).astype(bf16)
+        first = step * PROJ_ROWS
+        for at in range(first, first + PROJ_ROWS, PROJ_SUB):
+            value_ref[pl.ds(at, PROJ_SUB), :] = jnp.dot(
+                x_ref[pl.ds(at, PROJ_SUB), :], w_ref[...], preferred_element_type=f32
+            )
+            if at > first:
+                normalize(at - PROJ_SUB)
+        normalize(first + PROJ_ROWS - PROJ_SUB)
         for store in stores(step):
             store.start()
     for step in range(PROJ_STEPS):
@@ -146,41 +162,56 @@
     return pl.pallas_call(
         project_kernel,
         in_specs=[hbm, vmem],
-        out_specs=[hbm, hbm],
+        out_specs=[hbm, hbm, vmem],
         out_shape=[
-            jax.ShapeDtypeStruct((total, PROJ), f32),
             jax.ShapeDtypeStruct((total, PROJ), bf16),
+            jax.ShapeDtypeStruct((total, PROJ), bf16),
+            jax.ShapeDtypeStruct((total // 128, 128), f32),
         ],
         scratch_shapes=[
-            pltpu.VMEM((PROJ_SLOTS, PROJ_ROWS, D_FEAT), bf16),
+            pltpu.VMEM((total, D_FEAT), bf16),
             pltpu.VMEM((total, PROJ), f32),
             pltpu.VMEM((total, PROJ), bf16),
-            pltpu.SemaphoreType.DMA((PROJ_SLOTS,)),
+            pltpu.VMEM((total, PROJ), bf16),
+            pltpu.SemaphoreType.DMA((PROJ_STEPS,)),
             pltpu.SemaphoreType.DMA((PROJ_STEPS,)),
             pltpu.SemaphoreType.DMA((PROJ_STEPS,)),
         ],
         compiler_params=pltpu.CompilerParams(vmem_limit_bytes=58 * MIB),
         cost_estimate=pl.CostEstimate(
             flops=2 * total * D_FEAT * PROJ,
-            bytes_accessed=total * (2 * D_FEAT + 6 * PROJ),
+            bytes_accessed=total * (2 * D_FEAT + 4 * PROJ),
             transcendentals=0,
         ),
         name="project",
     )(rows, weight)
 
 
-def slot_columns(recv_ref):
+def receive(parts, recv_ref, sems):
+    half = CHIPS * QSTRIDE
+    copies = [
+        pltpu.make_async_copy(part, recv_ref.at[pl.ds(i * half, half)], sems.at[i])
+        for i, part in enumerate(parts)
+    ]
+    for copy in copies:
+        copy.start()
+    return copies
+
+
+def slot_columns(recv_ref, core):
     meta = recv_ref[...].reshape(OWNERS, QSTRIDE, PROJ)[:, QROWS:QSTRIDE, :].astype(f32)
     meta = meta[:, 0:SLOTS, :].reshape(ENTRIES, PROJ)
-    lane = iota((ENTRIES, PROJ), 1)
+    lane = iota((ENTRIES, PROJ), 1) - 2 * SLOTS * core
     slot = iota((ENTRIES, PROJ), 0) % SLOTS
     page = jnp.sum(jnp.where(lane == slot, meta, 0.0), axis=1, keepdims=True).astype(i32) - 1
     code = jnp.sum(jnp.where(lane == slot + SLOTS, meta, 0.0), axis=1, keepdims=True).astype(i32)
-    query = (iota((ENTRIES, 1), 0) // SLOTS) * QBLOCK + code // 2
-    return page, query, code % 2
-
-
-def plan_entries(page, query):
+    source = iota((ENTRIES, 1), 0) // SLOTS
+    other = source // CHIPS
+    owner = 2 * (source % CHIPS) + jnp.where(other == 0, core, 1 - core)
+    return page, owner * QBLOCK + code // 2, code // 2, code % 2
+
+
+def plan_entries(page, of_source):
     valid = page >= 0
     page_f = page.astype(f32)
     page_row = col_to_row(page_f, ENTRIES)
@@ -199,9 +230,10 @@
     at = position == iota((ENTRIES, POSITIONS), 1)
     entry_id = iota((ENTRIES, 1), 0)
     slot_row = jnp.sum(jnp.where(at, entry_id - ENTRIES, 0), axis=0, keepdims=True) + ENTRIES
-    row_of = (query // QBLOCK) * QSTRIDE + (query % QBLOCK) * QTOK
+    source = entry_id // SLOTS
+    row_of = source * QSTRIDE + of_source * QTOK
     row_row = jnp.sum(jnp.where(at, row_of, 0), axis=0, keepdims=True)
-    out_row = (query // QBLOCK) * RSTRIDE + (query % QBLOCK) * QTOK
+    out_row = source * QROWS + of_source * QTOK
     query_row = jnp.sum(jnp.where(at, out_row, 0), axis=0, keepdims=True)
     start_col = row_to_col(start, 128)[0:P_DEV]
     chunk_page = (
@@ -243,15 +275,20 @@
 
 
 def forward_kernel(
-    recv_ref, emb_hbm, back_ref, table_out, exps_ref, emb_ref, table_ref, logs_of, sims_ref, sems
+    core_ref, own_any, other_any, emb_hbm, back_ref, table_out, exps_ref,
+    recv_ref, emb_ref, table_ref, logs_of, sims_ref, sems, recv_sems,
 ):
     emb_copy = pltpu.make_async_copy(emb_hbm, emb_ref, sems.at[1])
+    core = core_ref[0]
+    received = receive((own_any, other_any), recv_ref, recv_sems)
     emb_copy.start()
-    page, query, positive = slot_columns(recv_ref)
-    table_out[...] = plan_entries(page, query)
+    sims_ref[...] = jnp.zeros(sims_ref.shape, f32)
+    for copy in received:
+        copy.wait()
+    page, query, of_source, positive = slot_columns(recv_ref, core)
+    table_out[...] = plan_entries(page, of_source)
     copy = pltpu.make_async_copy(table_out, table_ref, sems.at[0])
     copy.start()
-    sims_ref[...] = jnp.zeros(sims_ref.shape, f32)
     copy.wait()
     emb_copy.wait()
     group = iota((1, 128), 1) // QTOK
@@ -281,56 +318,68 @@
     spread = jnp.where(lane == slot, scores, 0.0).reshape(OWNERS, SLOTS, 128)
     spread = jnp.sum(spread, axis=1, keepdims=True)
     which = iota((OWNERS, SLOTS, 128), 1)
-    back_ref[...] = jnp.where(
-        which == 0, sums[None], jnp.where(which == 1, spread, 0.0)
-    )
-
-
-def forward(recv, emb):
+    result = jnp.where(which == 0, sums[None], jnp.where(which == 1, spread, 0.0))
+    own, other = result[0:CHIPS], result[CHIPS:OWNERS]
+    back_ref[:, 0] = jnp.where(core == 0, own, other)
+    back_ref[:, 1] = jnp.where(core == 0, other, own)
+
+
+def forward(core, own, other, emb):
     vmem = pl.BlockSpec(memory_space=pltpu.VMEM)
+    place = pl.BlockSpec(memory_space=pl.ANY)
     return pl.pallas_call(
         forward_kernel,
-        in_specs=[vmem, pl.BlockSpec(memory_space=pltpu.HBM)],
+        in_specs=[
+            pl.BlockSpec(memory_space=pltpu.SMEM),
+            place,
+            place,
+            pl.BlockSpec(memory_space=pltpu.HBM),
+        ],
         out_specs=[vmem, vmem, vmem],
         out_shape=[
-            jax.ShapeDtypeStruct((OWNERS, SLOTS, 128), f32),
+            jax.ShapeDtypeStruct((CHIPS, 2, SLOTS, 128), f32),
             jax.ShapeDtypeStruct((8, POSITIONS), i32),
             jax.ShapeDtypeStruct((ENTRIES, 128), f32),
         ],
         scratch_shapes=[
+            pltpu.VMEM((OWNERS * QSTRIDE, PROJ), bf16),
             pltpu.VMEM((P_DEV * TOKP, PROJ), bf16),
             pltpu.SMEM((8, POSITIONS), i32),
             pltpu.VMEM((ENTRIES + 8, 128), f32),
             pltpu.VMEM((2, TOKP, LANES), f32),
             pltpu.SemaphoreType.DMA((2,)),
+            pltpu.SemaphoreType.DMA((2,)),
         ],
         compiler_params=pltpu.CompilerParams(vmem_limit_bytes=58 * MIB),
         name="forward",
-    )(recv, emb)
-
-
-FEAT_STEPS = 10
-FEAT_SLOTS = 6
+    )(core, own, other, emb)
+
+
+FEAT_STEPS = 5
+FEAT_SUB = 1024
 FEAT_ROWS = P_DEV * TOKP // FEAT_STEPS
 
 
 def backward_kernel(
-    table_ref, recv_ref, exps_ref, sums_ref, emb_hbm, proj_hbm, feat_hbm, out_ref,
-    weight_of, page_acc, query_acc, emb_ref, proj_ref, grad_ref, feat_ref, sims_ref, grads_ref, sems,
+    core_ref, table_ref, exps_ref, sums_ref, scale_ref, own_any, other_any, emb_hbm, rest_hbm, feat_hbm,
+    keep_ref, give_ref, recv_ref, weight_of, page_acc, query_acc, emb_ref, rest_ref, grad_ref, feat_ref, sims_ref, grads_ref, sems, recv_sems,
 ):
     def feature_copy(step):
         part = pl.ds(step * FEAT_ROWS, FEAT_ROWS)
-        slot = step % FEAT_SLOTS
-        return pltpu.make_async_copy(feat_hbm.at[part], feat_ref.at[slot], sems.at[slot])
-
-    emb_copy = pltpu.make_async_copy(emb_hbm, emb_ref, sems.at[FEAT_SLOTS])
+        return pltpu.make_async_copy(feat_hbm.at[part], feat_ref.at[part], sems.at[step])
+
+    emb_copy = pltpu.make_async_copy(emb_hbm, emb_ref, sems.at[FEAT_STEPS])
+    received = receive((own_any, other_any), recv_ref, recv_sems)
     emb_copy.start()
-    proj_copy = pltpu.make_async_copy(proj_hbm, proj_ref, sems.at[FEAT_SLOTS + 1])
-    proj_copy.start()
-    for step in range(FEAT_SLOTS):
-        feature_copy(step).start()
-
-    page, query, positive = slot_columns(recv_ref)
+    rest_copy = pltpu.make_async_copy(rest_hbm, rest_ref, sems.at[FEAT_STEPS + 1])
+
+    page_acc[...] = jnp.zeros(page_acc.shape, f32)
+    query_acc[...] = jnp.zeros(query_acc.shape, f32)
+    sims_ref[...] = jnp.zeros(sims_ref.shape, f32)
+    grads_ref[...] = jnp.zeros(grads_ref.shape, bf16)
+    for copy in received:
+        copy.wait()
+    page, query, of_source, positive = slot_columns(recv_ref, core_ref[0])
     sums = jnp.sum(sums_ref[...], axis=0)[0:1]
     lane = iota((ENTRIES, 128), 1)
     total = jnp.sum(jnp.where(query == lane, sums, 0.0), axis=1, keepdims=True)
@@ -340,11 +389,10 @@
         valid, exps_ref[...] / total - positive.astype(f32), 0.0
     )
     weight_of[ENTRIES : ENTRIES + 8, :] = jnp.zeros((8, 128), f32)
-    page_acc[...] = jnp.zeros(page_acc.shape, f32)
-    query_acc[...] = jnp.zeros(query_acc.shape, f32)
-    sims_ref[...] = jnp.zeros(sims_ref.shape, f32)
-    grads_ref[...] = jnp.zeros(grads_ref.shape, bf16)
     emb_copy.wait()
+    rest_copy.start()
+    for step in range(FEAT_STEPS):
+        feature_copy(step).start()
     group = iota((1, 128), 1) // QTOK
 
     def chunk_weights(chunk):
@@ -382,58 +430,82 @@
         return carry
 
     lax.fori_loop(0, (table_ref[3, 128] + 2 + UNROLL - 1) // UNROLL, steps, 0)
-    out_ref[:, 0:QROWS, :] = query_acc[...].astype(bf16).reshape(OWNERS, QROWS, PROJ)
-    proj_copy.wait()
-
-    def token_grads(step, carry):
-        part = pl.ds(pl.multiple_of(step * 512, 512), 512)
-        value = proj_ref[part, :]
-        upstream = page_acc[part, :]
-        scale = lax.rsqrt(jnp.sum(value * value, axis=1, keepdims=True) + epsilon)
-        inner = jnp.sum(value * upstream, axis=1, keepdims=True)
-        grad_ref[part, :] = (
-            upstream * scale - value * (scale * scale * scale * inner)
-        ).astype(bf16)
-        return carry
-
-    lax.fori_loop(0, P_DEV * TOKP // 512, token_grads, 0)
+    half = CHIPS * QROWS
+    for ref, at in ((keep_ref, 0), (give_ref, half)):
+        ref[:, 0:QROWS, :] = query_acc[at : at + half, :].astype(bf16).reshape(CHIPS, QROWS, PROJ)
+    rest_copy.wait()
+
+    def token_grads(at):
+        for block in range(at // 128, (at + FEAT_SUB) // 128):
+            part = pl.ds(block * 128, 128)
+            unit = emb_ref[part, :].astype(f32) + rest_ref[part, :].astype(f32)
+            upstream = page_acc[part, :]
+            scale = row_to_col(scale_ref[block : block + 1, :], 128)
+            inner = jnp.sum(unit * upstream, axis=1, keepdims=True)
+            grad_ref[part, :] = (scale * (upstream - unit * inner)).astype(bf16)
+
+    total = P_DEV * TOKP
     grad = jnp.zeros((PROJ, D_FEAT), f32)
-    for step in range(FEAT_STEPS):
-        part = pl.ds(step * FEAT_ROWS, FEAT_ROWS)
-        feature_copy(step).wait()
-        grad += contract_first(grad_ref[part, :], feat_ref[step % FEAT_SLOTS])
-        if step + FEAT_SLOTS < FEAT_STEPS:
-            feature_copy(step + FEAT_SLOTS).start()
+    token_grads(0)
+    for at in range(0, total, FEAT_SUB):
+        if at % FEAT_ROWS == 0:
+            feature_copy(at // FEAT_ROWS).wait()
+        if at + FEAT_SUB < total:
+            token_grads(at + FEAT_SUB)
+        part = pl.ds(at, FEAT_SUB)
+        grad += contract_first(grad_ref[part, :], feat_ref[part, :])
     grad = grad.T
-    for owner in range(OWNERS):
-        rows = grad[owner * GRAD_ROWS : (owner + 1) * GRAD_ROWS]
-        rows = jnp.concatenate([rows, jnp.zeros((GRAD_PAD - GRAD_ROWS, PROJ), f32)], axis=0)
-        out_ref[owner, QROWS : QROWS + GRAD_PAD, :] = rows.astype(bf16)
-
-
-def backward(table, recv, exps, sums, emb, proj, rows):
+    pad = jnp.zeros((GRAD_PAD - GRAD_ROWS, PROJ), f32)
+    first_core = core_ref[0] == 0
+    for chip in range(CHIPS):
+        at = 2 * chip * GRAD_ROWS
+        even = jnp.concatenate([grad[at : at + GRAD_ROWS], pad], axis=0)
+        odd = jnp.concatenate([grad[at + GRAD_ROWS : at + 2 * GRAD_ROWS], pad], axis=0)
+        rows = pl.ds(QROWS, GRAD_PAD)
+        keep_ref[chip, rows, :] = jnp.where(first_core, even, odd).astype(bf16)
+        give_ref[chip, rows, :] = jnp.where(first_core, odd, even).astype(bf16)
+
+
+def backward(core, table, exps, sums, scale, own, other, emb, rest, rows):
     vmem = pl.BlockSpec(memory_space=pltpu.VMEM)
     hbm = pl.BlockSpec(memory_space=pltpu.HBM)
+    smem = pl.BlockSpec(memory_space=pltpu.SMEM)
+    place = pl.BlockSpec(memory_space=pl.ANY)
     return pl.pallas_call(
         backward_kernel,
-        in_specs=[pl.BlockSpec(memory_space=pltpu.SMEM), vmem, vmem, vmem, hbm, hbm, hbm],
-        out_specs=vmem,
-        out_shape=jax.ShapeDtypeStruct((OWNERS, QROWS + GRAD_PAD, PROJ), bf16),
+        in_specs=[smem, smem, vmem, vmem, vmem, place, place, hbm, hbm, hbm],
+        out_specs=[vmem, vmem],
+        out_shape=[jax.ShapeDtypeStruct((CHIPS, QROWS + GRAD_PAD, PROJ), bf16)] * 2,
         scratch_shapes=[
+            pltpu.VMEM((OWNERS * QSTRIDE, PROJ), bf16),
             pltpu.VMEM((ENTRIES + 8, 128), f32),
             pltpu.VMEM((P_DEV * TOKP, PROJ), f32),
             pltpu.VMEM((OWNERS * QROWS, PROJ), f32),
             pltpu.VMEM((P_DEV * TOKP, PROJ), bf16),
-            pltpu.VMEM((P_DEV * TOKP, PROJ), f32),
             pltpu.VMEM((P_DEV * TOKP, PROJ), bf16),
-            pltpu.VMEM((FEAT_SLOTS, FEAT_ROWS, D_FEAT), bf16),
+            pltpu.VMEM((P_DEV * TOKP, PROJ), bf16),
+            pltpu.VMEM((P_DEV * TOKP, D_FEAT), bf16),
             pltpu.VMEM((2, TOKP, LANES), f32),
             pltpu.VMEM((2, TOKP, LANES), bf16),
-            pltpu.SemaphoreType.DMA((FEAT_SLOTS + 2,)),
+            pltpu.SemaphoreType.DMA((FEAT_STEPS + 2,)),
+            pltpu.SemaphoreType.DMA((2,)),
         ],
         compiler_params=pltpu.CompilerParams(vmem_limit_bytes=58 * MIB),
         name="backward",
-    )(table, recv, exps, sums, emb, proj, rows)
+    )(core, table, exps, sums, scale, own, other, emb, rest, rows)
+
+
+def pair_kernel(a_ref, b_ref, out_ref):
+    out_ref[...] = (a_ref[...].astype(f32) + b_ref[...].astype(f32)).astype(bf16)
+
+
+def pair_sum(a, b):
+    return pl.pallas_call(
+        pair_kernel,
+        out_shape=jax.ShapeDtypeStruct(a.shape, bf16),
+        compiler_params=SMALL,
+        name="pair_sum",
+    )(a, b)
 
 
 def share_kernel(parts_ref, out_ref):
@@ -506,17 +578,27 @@
     return jnp.sum(jnp.where(pick, slots[None], 0.0), axis=(1, 2)).reshape(page_ids.shape)
 
 
-def exchange(values, axes):
-    return lax.all_to_all(values, axes, split_axis=0, concat_axis=0, tiled=True)
+def exchange(values, axes, groups=None):
+    return lax.all_to_all(
+        values, axes, split_axis=0, concat_axis=0, axis_index_groups=groups, tiled=True
+    )
 
 
 def per_device(features, queries, proj_weight, page_ids):
     rows = features.reshape(P_DEV * TOKP, D_FEAT)
-    recv = exchange(send_queries(page_ids, queries), "pages").reshape(OWNERS * QSTRIDE, PROJ)
-    proj, emb = project(rows, proj_weight)
-    back, table, exps = forward(recv, emb)
-    sums = exchange(back, "pages")
-    parts = exchange(backward(table, recv, exps, sums, emb, proj, rows), "pages")
+    same_core = [list(range(first, OWNERS, 2)) for first in range(2)]
+    other_core = [(i, i ^ 1) for i in range(OWNERS)]
+    core = (lax.axis_index("pages") % 2).astype(i32).reshape(1)
+    own = exchange(send_queries(page_ids, queries), "pages", same_core)
+    own, emb, rest, scale = lax.optimization_barrier((own, *project(rows, proj_weight)))
+    other = lax.ppermute(own, "pages", other_core)
+    own = own.reshape(CHIPS * QSTRIDE, PROJ)
+    other = other.reshape(CHIPS * QSTRIDE, PROJ)
+    back, table, exps = forward(core, own, other, emb)
+    sums = exchange(back.reshape(OWNERS, SLOTS, 128), "pages")
+    keep, give = backward(core, table, exps, sums, scale, own, other, emb, rest, rows)
+    taken = lax.ppermute(give, "pages", other_core)
+    parts = exchange(pair_sum(keep, taken), "pages", same_core)
     share = own_share(parts)
     replicas = lax.axis_size("rep")
     shares = [share] + [

time: 128 us -> 115 us (0.90)
  Pallas kernels: 45.4 us -> 39.3 us
  waiting for transfers between devices: 32.7 us -> 27.6 us
    all_to_all x3, waiting for transfers between devices: 28.7 us -> 20.1 us  [exchange(): lax.all_to_all(values, axes, split_axis=0, concat_axis=0, axis_index_grou...]
    pallas_call x4 -> x5, Pallas kernels: 42.8 us -> 36.8 us  [the longest x1 15.1 us: backward(): pl.pallas_call(backward_kernel, in_specs=[smem, smem, vmem, vmem, vmem, p...]
    ppermute x0 -> x2, waiting for transfers between devices: none -> 3.66 us  [the longest x1 2.03 us: per_device(): taken = lax.ppermute(give, 'pages', other_core)]
    all_to_all x3, starting transfers between devices: 23 us -> 20.2 us  [exchange(): lax.all_to_all(values, axes, split_axis=0, concat_axis=0, axis_index_grou...]
    ppermute x0 -> x2, starting transfers between devices: none -> 1.52 us  [the longest x1 1.03 us: per_device(): other = lax.ppermute(own, 'pages', other_core)]
  transfers between devices with their start and end apart: 6 -> 8, of which waited for: 5 -> 6; matrix products, arithmetic and copies ran while one was open for 2% -> 2% of each run, Pallas kernels for 14% -> 12%
where the time goes in v3:
time: 115 us
  Pallas kernels  39.3 us (34%)
  waiting for transfers between devices  27.6 us (24%)
  starting transfers between devices  26.5 us (23%)
  blocking collectives  16.2 us (14%)
  local copies, waits for them, and re-layouts  3.79 us (3%)
    all_to_all x3, starting transfers between devices, exchange(): lax.all_to_all(values, axes, split_axis=0, concat_axis=0, axis_index_grou...  20.2 us
    all_to_all x3, waiting for transfers between devices, exchange(): lax.all_to_all(values, axes, split_axis=0, concat_axis=0, axis_index_grou...  20.1 us
    all_to_all x1, blocking collectives, exchange(): lax.all_to_all(values, axes, split_axis=0, concat_axis=0, axis_index_grou...  16.2 us
    pallas_call x1, Pallas kernels, backward(): pl.pallas_call(backward_kernel, in_specs=[smem, smem, vmem, vmem, vmem, p...  15.1 us
    pallas_call x1, Pallas kernels, project(): pl.pallas_call(project_kernel, in_specs=[hbm, vmem], out_specs=[hbm, hbm,...  13.1 us
    pallas_call x1, Pallas kernels, forward(): pl.pallas_call(forward_kernel, in_specs=[pl.BlockSpec(memory_space=pltpu....  5.46 us
    ppermute x3, starting transfers between devices, per_device(): lax.ppermute(share, 'rep', [(i, i ^ k) for i in range(replicas)])  4.77 us
    ppermute x3, waiting for transfers between devices, per_device(): lax.ppermute(share, 'rep', [(i, i ^ k) for i in range(replicas)])  3.81 us
  transfers between devices with their start and end apart: 8, of which 6 were waited for; matrix products, arithmetic and copies ran while one was open for 2% of the time, Pallas kernels for 12%

profile of v3, /device:TPU:1, one launch (start us, length us, event | category | flops | bytes accessed | tf_op | source)
XLA Modules:
  0.0 114.6 jit_solution(7355575042222742555)
XLA Ops:
  0.6 2.2 %send_queries.1 = bf16[16,144,128]{2,1,0:T(8,128)(2,1)} custom-call(s32[4,16]{1,0:T(4,128)} %ids_ref.1, bf16[4,32,128]{2,1,0:T(8,128)(2,1)} %q_ref.3), custom_call_target="tpu_custom_call" | custom-call | tf_op jit(solution)/shard_map/send_queries/pallas_call | solution.py:99
  2.8 7.6 %all-to-all-start = ((bf16[16,144,128]{2,1,0:T(8,128)(2,1)}), bf16[16,144,128]{2,1,0:T(8,128)(2,1)S(1)}, u32[]{:S(2)}, u32[]{:S(2)}) async-start(bf16[16,144,128]{2,1,0:T(8,128)(2,1)} %send_queries.1), calls=%async_computation | async-start | bytes 1179648 | tf_op jit(solution)/shard_map/all_to_all | solution.py:582
  10.4 13.1 %project.1 = (bf16[10240,128]{1,0:T(8,128)(2,1)}, bf16[10240,128]{1,0:T(8,128)(2,1)}, f32[80,128]{1,0:T(8,128)}) custom-call(bf16[10240,1152]{1,0:T(8,128)(2,1)} %bitcast.6, bf16[1152,128]{1,0:T(8,128)(2,1)} %w_ref.1), custom_call_target="tpu_custom_call" | custom-call | flops 3019898880 | bytes 28835840 | tf_op jit(solution)/shard_map/project/pallas_call | solution.py:162
  23.5 0.0 all-to-all-done
  23.5 0.0 copy-start.2
  23.5 1.0 collective-permute-start
  24.6 1.6 %collective-permute-done = bf16[16,144,128]{2,1,0:T(8,128)(2,1)S(1)} collective-permute-done((bf16[16,144,128]{2,1,0:T(8,128)(2,1)S(1)}, bf16[16,144,128]{2,1,0:T(8,128)(2,1)S(1)}, u32[]{:S(2)}, u32[]{:S(2)}) %collective-permute-start) | collective-permute-done | bytes 589856 | tf_op jit(solution)/shard_map/ppermute | solution.py:594
  26.2 0.0 copy-start.3
  26.2 0.0 copy-done.2
  26.2 0.8 copy-done.3
  27.0 5.5 %forward.1 = (f32[16,2,8,128]{3,2,1,0:T(8,128)}, s32[8,640]{1,0:T(8,128)}, f32[256,128]{1,0:T(8,128)}) custom-call(s32[1]{0:T(128)} %bitcast.core_ref, bf16[2304,128]{1,0:T(8,128)(2,1)} %bitcast.8, bf16[2304,128]{1,0:T(8,128)(2,1)} %bitcast.10, bf16[10240,128]{1,0:T(8,128)(2,1)} %get-tuple-element.19.emb_hbm), custom_call_target="tpu_custom_call" | custom-call | tf_op jit(solution)/shard_map/forward/pallas_call | solution.py:330
  32.5 16.2 %all_to_all.20.sums_ref = f32[32,8,128]{2,1,0:T(8,128)} all-to-all(f32[32,8,128]{2,1,0:T(8,128)} %bitcast.12), channel_id=1, replica_groups=mesh['pages'=32,'rep'=4] {'pages'}, dimensions={0} | all-to-all | bytes 262144 | tf_op jit(solution)/shard_map/all_to_all | solution.py:582
  48.7 15.1 %backward.1 = (bf16[16,176,128]{2,1,0:T(8,128)(2,1)}, bf16[16,176,128]{2,1,0:T(8,128)(2,1)}) custom-call(s32[1]{0:T(128)} %bitcast.core_ref, s32[8,640]{1,0:T(8,128)} %get-tuple-element.21.table_ref, f32[256,128]{1,0:T(8,128)} %get-tuple-element.22.exps_ref, f32[32,8,128]{2,1,0:T(8,128)} %all_to_all.20.sums_ref, f32[80,128]{1,0:T(8,128)} %get-tuple-element.23.scale_ref, ...), custom_call_target="tpu_custom_call" | custom-call | tf_op jit(solution)/shard_map/backward/pallas_call | solution.py:474
  63.7 0.0 copy-start.4
  63.8 0.5 collective-permute-start.1
  64.2 2.0 %collective-permute-done.1.b_ref = bf16[16,176,128]{2,1,0:T(8,128)(2,1)S(1)} collective-permute-done((bf16[16,176,128]{2,1,0:T(8,128)(2,1)}, bf16[16,176,128]{2,1,0:T(8,128)(2,1)S(1)}, u32[]{:S(2)}, u32[]{:S(2)}) %collective-permute-start.1) | collective-permute-done | bytes 720928 | tf_op jit(solution)/shard_map/ppermute | solution.py:600
  66.3 0.0 copy-start
  66.3 1.1 copy-done
  67.4 0.0 copy-start.1
  67.4 1.0 pair_sum.1
  68.4 5.7 %all-to-all-start.2 = ((bf16[16,176,128]{2,1,0:T(8,128)(2,1)}), bf16[16,176,128]{2,1,0:T(8,128)(2,1)S(1)}, u32[]{:S(2)}, u32[]{:S(2)}) async-start(bf16[16,176,128]{2,1,0:T(8,128)(2,1)} %pair_sum.1), calls=%async_computation.2 | async-start | bytes 1441792 | tf_op jit(solution)/shard_map/all_to_all | solution.py:582
  74.2 0.0 copy-done.4
  74.2 0.1 div.14
  74.3 0.1 and.31
  74.4 0.1 broadcast_compare_fusion
  74.5 0.1 reduce_window_sum.11
  74.6 12.4 %all-to-all-done.2.parts_ref = bf16[16,176,128]{2,1,0:T(8,128)(2,1)S(1)} async-done(((bf16[16,176,128]{2,1,0:T(8,128)(2,1)}), bf16[16,176,128]{2,1,0:T(8,128)(2,1)S(1)}, u32[]{:S(2)}, u32[]{:S(2)}) %all-to-all-start.2) | async-done | bytes 720928 | tf_op jit(solution)/shard_map/all_to_all | solution.py:582
  87.0 1.7 %collective-permute-start.2 = (f32[48,128]{1,0:T(8,128)S(1)}, f32[48,128]{1,0:T(8,128)S(1)}, u32[]{:S(2)}, u32[]{:S(2)}) collective-permute-start(f32[48,128]{1,0:T(8,128)S(1)} %own_share.1.a_ref), channel_id=1, source_target_pairs={{0,1},{1,0},{2,3},{3,2},{4,5},{5,4},{6,7},{7,6},{8,9},{9,8},{10,11... | collective-permute-start | bytes 73736 | tf_op jit(solution)/shard_map/ppermute | solution.py:605
  88.7 3.1 %collective-permute-start.3 = (f32[48,128]{1,0:T(8,128)S(1)}, f32[48,128]{1,0:T(8,128)S(1)}, u32[]{:S(2)}, u32[]{:S(2)}) collective-permute-start(f32[48,128]{1,0:T(8,128)S(1)} %own_share.1.a_ref), channel_id=1, source_target_pairs={{0,2},{1,3},{2,0},{3,1},{4,6},{5,7},{6,4},{7,5},{8,10},{9,11},{10,... | collective-permute-start | bytes 73736 | tf_op jit(solution)/shard_map/ppermute | solution.py:605
  91.8 0.0 collective-permute-start.4
  91.8 0.2 select_reduce_fusion.1
  92.0 0.0 collective-permute-done.2.b_ref
  92.0 1.3 %collective-permute-done.3.c_ref = f32[48,128]{1,0:T(8,128)S(1)} collective-permute-done((f32[48,128]{1,0:T(8,128)S(1)}, f32[48,128]{1,0:T(8,128)S(1)}, u32[]{:S(2)}, u32[]{:S(2)}) %collective-permute-start.3) | collective-permute-done | bytes 24608 | tf_op jit(solution)/shard_map/ppermute | solution.py:605
  93.3 2.5 %collective-permute-done.4.d_ref = f32[48,128]{1,0:T(8,128)S(1)} collective-permute-done((f32[48,128]{1,0:T(8,128)S(1)}, f32[48,128]{1,0:T(8,128)S(1)}, u32[]{:S(2)}, u32[]{:S(2)}) %collective-permute-start.4) | collective-permute-done | bytes 24608 | tf_op jit(solution)/shard_map/ppermute | solution.py:605
  95.8 0.8 spread_share.1
  96.6 6.9 %all-to-all-start.3 = ((bf16[32,48,128]{2,1,0:T(8,128)(2,1)}), bf16[32,48,128]{2,1,0:T(8,128)(2,1)S(1)}, u32[]{:S(2)}, u32[]{:S(2)}) async-start(bf16[32,48,128]{2,1,0:T(8,128)(2,1)} %spread_share.1), calls=%async_computation.3 | async-start | bytes 786432 | tf_op jit(solution)/shard_map/all_to_all | solution.py:582
  103.5 0.1 copy.7
  103.6 0.9 slice.4
  104.5 0.1 select_reduce_fusion
  104.6 0.7 reshape.101
  105.3 0.0 copy-done.1
  105.3 0.8 query_grads.1
  106.1 7.7 %all-to-all-done.3.parts_ref = bf16[32,48,128]{2,1,0:T(8,128)(2,1)S(1)} async-done(((bf16[32,48,128]{2,1,0:T(8,128)(2,1)}), bf16[32,48,128]{2,1,0:T(8,128)(2,1)S(1)}, u32[]{:S(2)}, u32[]{:S(2)}) %all-to-all-start.3) | async-done | bytes 393248 | tf_op jit(solution)/shard_map/all_to_all | solution.py:582
  113.7 0.9 collect.1
  (6 shorter events, 0.1 us)
Async XLA Ops:
  2.8 20.7 %all-to-all-start = ((bf16[16,144,128]{2,1,0:T(8,128)(2,1)}), bf16[16,144,128]{2,1,0:T(8,128)(2,1)S(1)}, u32[]{:S(2)}, u32[]{:S(2)}) async-start(bf16[16,144,128]{2,1,0:T(8,128)(2,1)} %send_queries.1), calls=%async_computation | async-start | bytes 1179648 | tf_op jit(solution)/shard_map/all_to_all | solution.py:582
  23.5 2.7 %copy-start.2 = (bf16[16,144,128]{2,1,0:T(8,128)(2,1)}, bf16[16,144,128]{2,1,0:T(8,128)(2,1)S(1)}, u32[]{:S(2)}) copy-start(bf16[16,144,128]{2,1,0:T(8,128)(2,1)S(1)} %all-to-all-done) | copy-start | bytes 1769476
  23.5 2.7 %collective-permute-start = (bf16[16,144,128]{2,1,0:T(8,128)(2,1)S(1)}, bf16[16,144,128]{2,1,0:T(8,128)(2,1)S(1)}, u32[]{:S(2)}, u32[]{:S(2)}) collective-permute-start(bf16[16,144,128]{2,1,0:T(8,128)(2,1)S(1)} %all-to-all-done), channel_id=1, source_target_pairs={{0,4},{4,0},{8,12},{12,8},{16,20},{20,16},{24,28},{28,24},{32,36},... | collective-permute-start | bytes 1769480 | tf_op jit(solution)/shard_map/ppermute | solution.py:594
  26.2 0.8 copy-start.3
  63.7 10.4 %copy-start.4 = (s32[4,16]{1,0:T(4,128)S(1)}, s32[4,16]{1,0:T(4,128)}, u32[]{:S(2)}) copy-start(s32[4,16]{1,0:T(4,128)} %ids_ref.1) | copy-start | bytes 772
  63.8 2.5 %collective-permute-start.1 = (bf16[16,176,128]{2,1,0:T(8,128)(2,1)}, bf16[16,176,128]{2,1,0:T(8,128)(2,1)S(1)}, u32[]{:S(2)}, u32[]{:S(2)}) collective-permute-start(bf16[16,176,128]{2,1,0:T(8,128)(2,1)} %get-tuple-element.26), channel_id=1, source_target_pairs={{0,4},{4,0},{8,12},{12,8},{16,20},{20,16},{24,28},{28,24},{32,36},... | collective-permute-start | bytes 2162696 | tf_op jit(solution)/shard_map/ppermute | solution.py:600
  66.3 1.1 copy-start
  67.4 37.9 %copy-start.1 = (bf16[4,32,128]{2,1,0:T(8,128)(2,1)S(1)}, bf16[4,32,128]{2,1,0:T(8,128)(2,1)}, u32[]{:S(2)}) copy-start(bf16[4,32,128]{2,1,0:T(8,128)(2,1)} %q_ref.3) | copy-start | bytes 98308
  68.4 18.6 %all-to-all-start.2 = ((bf16[16,176,128]{2,1,0:T(8,128)(2,1)}), bf16[16,176,128]{2,1,0:T(8,128)(2,1)S(1)}, u32[]{:S(2)}, u32[]{:S(2)}) async-start(bf16[16,176,128]{2,1,0:T(8,128)(2,1)} %pair_sum.1), calls=%async_computation.2 | async-start | bytes 1441792 | tf_op jit(solution)/shard_map/all_to_all | solution.py:582
  87.0 4.9 %collective-permute-start.2 = (f32[48,128]{1,0:T(8,128)S(1)}, f32[48,128]{1,0:T(8,128)S(1)}, u32[]{:S(2)}, u32[]{:S(2)}) collective-permute-start(f32[48,128]{1,0:T(8,128)S(1)} %own_share.1.a_ref), channel_id=1, source_target_pairs={{0,1},{1,0},{2,3},{3,2},{4,5},{5,4},{6,7},{7,6},{8,9},{9,8},{10,11... | collective-permute-start | bytes 73736 | tf_op jit(solution)/shard_map/ppermute | solution.py:605
  88.7 4.5 %collective-permute-start.3 = (f32[48,128]{1,0:T(8,128)S(1)}, f32[48,128]{1,0:T(8,128)S(1)}, u32[]{:S(2)}, u32[]{:S(2)}) collective-permute-start(f32[48,128]{1,0:T(8,128)S(1)} %own_share.1.a_ref), channel_id=1, source_target_pairs={{0,2},{1,3},{2,0},{3,1},{4,6},{5,7},{6,4},{7,5},{8,10},{9,11},{10,... | collective-permute-start | bytes 73736 | tf_op jit(solution)/shard_map/ppermute | solution.py:605
  91.8 4.0 %collective-permute-start.4 = (f32[48,128]{1,0:T(8,128)S(1)}, f32[48,128]{1,0:T(8,128)S(1)}, u32[]{:S(2)}, u32[]{:S(2)}) collective-permute-start(f32[48,128]{1,0:T(8,128)S(1)} %own_share.1.a_ref), channel_id=1, source_target_pairs={{0,3},{1,2},{2,1},{3,0},{4,7},{5,6},{6,5},{7,4},{8,11},{9,10},{10,... | collective-permute-start | bytes 73736 | tf_op jit(solution)/shard_map/ppermute | solution.py:605
  96.6 17.2 %all-to-all-start.3 = ((bf16[32,48,128]{2,1,0:T(8,128)(2,1)}), bf16[32,48,128]{2,1,0:T(8,128)(2,1)S(1)}, u32[]{:S(2)}, u32[]{:S(2)}) async-start(bf16[32,48,128]{2,1,0:T(8,128)(2,1)} %spread_share.1), calls=%async_computation.3 | async-start | bytes 786432 | tf_op jit(solution)/shard_map/all_to_all | solution.py:582

commit v4 on v3

--- a/solution.py
+++ b/solution.py
@@ -105,33 +105,24 @@
 
 
 PROJ_ROWS = 2048
-PROJ_SUB = 512
+PROJ_SUB = 256
 PROJ_STEPS = P_DEV * TOKP // PROJ_ROWS
 
 
 def project_kernel(
-    x_hbm, w_ref, emb_hbm, rest_hbm, scale_out, x_ref, value_ref, emb_ref, rest_ref, sems, emb_sems, rest_sems
+    x_hbm, w_ref, emb_ref, scale_out, x_ref, value_ref, sems
 ):
     def part(step):
         return pl.ds(step * PROJ_ROWS, PROJ_ROWS)
 
     def load(step):
         return pltpu.make_async_copy(x_hbm.at[part(step)], x_ref.at[part(step)], sems.at[step])
-
-    def stores(step):
-        return (
-            pltpu.make_async_copy(emb_ref.at[part(step)], emb_hbm.at[part(step)], emb_sems.at[step]),
-            pltpu.make_async_copy(rest_ref.at[part(step)], rest_hbm.at[part(step)], rest_sems.at[step]),
-        )
 
     def normalize(at):
         rows = pl.ds(at, PROJ_SUB)
         value = value_ref[rows, :]
         scale = lax.rsqrt(jnp.sum(value * value, axis=1, keepdims=True) + epsilon)
-        unit = value * scale
-        emb = unit.astype(bf16)
-        emb_ref[rows, :] = emb
-        rest_ref[rows, :] = (unit - emb.astype(f32)).astype(bf16)
+        emb_ref[rows, :] = (value * scale).astype(bf16)
         for block in range(PROJ_SUB // 128):
             row = at // 128 + block
             scale_out[row : row + 1, :] = col_to_row(scale[block * 128 : block * 128 + 128], 128)
@@ -148,11 +139,6 @@
             if at > first:
                 normalize(at - PROJ_SUB)
         normalize(first + PROJ_ROWS - PROJ_SUB)
-        for store in stores(step):
-            store.start()
-    for step in range(PROJ_STEPS):
-        for store in stores(step):
-            store.wait()
 
 
 def project(rows, weight):
@@ -162,25 +148,20 @@
     return pl.pallas_call(
         project_kernel,
         in_specs=[hbm, vmem],
-        out_specs=[hbm, hbm, vmem],
+        out_specs=[vmem, vmem],
         out_shape=[
-            jax.ShapeDtypeStruct((total, PROJ), bf16),
             jax.ShapeDtypeStruct((total, PROJ), bf16),
             jax.ShapeDtypeStruct((total // 128, 128), f32),
         ],
         scratch_shapes=[
             pltpu.VMEM((total, D_FEAT), bf16),
             pltpu.VMEM((total, PROJ), f32),
-            pltpu.VMEM((total, PROJ), bf16),
-            pltpu.VMEM((total, PROJ), bf16),
-            pltpu.SemaphoreType.DMA((PROJ_STEPS,)),
-            pltpu.SemaphoreType.DMA((PROJ_STEPS,)),
             pltpu.SemaphoreType.DMA((PROJ_STEPS,)),
         ],
-        compiler_params=pltpu.CompilerParams(vmem_limit_bytes=58 * MIB),
+        compiler_params=pltpu.CompilerParams(vmem_limit_bytes=36 * MIB),
         cost_estimate=pl.CostEstimate(
             flops=2 * total * D_FEAT * PROJ,
-            bytes_accessed=total * (2 * D_FEAT + 4 * PROJ),
+            bytes_accessed=total * (2 * D_FEAT + 2 * PROJ),
             transcendentals=0,
         ),
         name="project",
@@ -275,13 +256,11 @@
 
 
 def forward_kernel(
-    core_ref, own_any, other_any, emb_hbm, back_ref, table_out, exps_ref,
-    recv_ref, emb_ref, table_ref, logs_of, sims_ref, sems, recv_sems,
+    core_ref, own_any, other_any, emb_ref, back_ref, table_out, exps_ref,
+    recv_ref, table_ref, logs_of, sims_ref, sems, recv_sems,
 ):
-    emb_copy = pltpu.make_async_copy(emb_hbm, emb_ref, sems.at[1])
     core = core_ref[0]
     received = receive((own_any, other_any), recv_ref, recv_sems)
-    emb_copy.start()
     sims_ref[...] = jnp.zeros(sims_ref.shape, f32)
     for copy in received:
         copy.wait()
@@ -290,7 +269,6 @@
     copy = pltpu.make_async_copy(table_out, table_ref, sems.at[0])
     copy.start()
     copy.wait()
-    emb_copy.wait()
     group = iota((1, 128), 1) // QTOK
 
     def steps(step, carry):
@@ -333,7 +311,7 @@
             pl.BlockSpec(memory_space=pltpu.SMEM),
             place,
             place,
-            pl.BlockSpec(memory_space=pltpu.HBM),
+            vmem,
         ],
         out_specs=[vmem, vmem, vmem],
         out_shape=[
@@ -343,14 +321,13 @@
         ],
         scratch_shapes=[
             pltpu.VMEM((OWNERS * QSTRIDE, PROJ), bf16),
-            pltpu.VMEM((P_DEV * TOKP, PROJ), bf16),
             pltpu.SMEM((8, POSITIONS), i32),
             pltpu.VMEM((ENTRIES + 8, 128), f32),
             pltpu.VMEM((2, TOKP, LANES), f32),
             pltpu.SemaphoreType.DMA((2,)),
             pltpu.SemaphoreType.DMA((2,)),
         ],
-        compiler_params=pltpu.CompilerParams(vmem_limit_bytes=58 * MIB),
+        compiler_params=pltpu.CompilerParams(vmem_limit_bytes=16 * MIB),
         name="forward",
     )(core, own, other, emb)
 
@@ -361,17 +338,14 @@
 
 
 def backward_kernel(
-    core_ref, table_ref, exps_ref, sums_ref, scale_ref, own_any, other_any, emb_hbm, rest_hbm, feat_hbm,
-    keep_ref, give_ref, recv_ref, weight_of, page_acc, query_acc, emb_ref, rest_ref, grad_ref, feat_ref, sims_ref, grads_ref, sems, recv_sems,
+    core_ref, table_ref, exps_ref, sums_ref, scale_ref, own_any, other_any, emb_ref, feat_hbm,
+    keep_ref, give_ref, recv_ref, weight_of, page_acc, query_acc, grad_ref, feat_ref, sims_ref, grads_ref, sems, recv_sems,
 ):
     def feature_copy(step):
         part = pl.ds(step * FEAT_ROWS, FEAT_ROWS)
         return pltpu.make_async_copy(feat_hbm.at[part], feat_ref.at[part], sems.at[step])
 
-    emb_copy = pltpu.make_async_copy(emb_hbm, emb_ref, sems.at[FEAT_STEPS])
     received = receive((own_any, other_any), recv_ref, recv_sems)
-    emb_copy.start()
-    rest_copy = pltpu.make_async_copy(rest_hbm, rest_ref, sems.at[FEAT_STEPS + 1])
 
     page_acc[...] = jnp.zeros(page_acc.shape, f32)
     query_acc[...] = jnp.zeros(query_acc.shape, f32)
@@ -389,8 +363,6 @@
         valid, exps_ref[...] / total - positive.astype(f32), 0.0
     )
     weight_of[ENTRIES : ENTRIES + 8, :] = jnp.zeros((8, 128), f32)
-    emb_copy.wait()
-    rest_copy.start()
     for step in range(FEAT_STEPS):
         feature_copy(step).start()
     group = iota((1, 128), 1) // QTOK
@@ -433,12 +405,11 @@
     half = CHIPS * QROWS
     for ref, at in ((keep_ref, 0), (give_ref, half)):
         ref[:, 0:QROWS, :] = query_acc[at : at + half, :].astype(bf16).reshape(CHIPS, QROWS, PROJ)
-    rest_copy.wait()
 
     def token_grads(at):
         for block in range(at // 128, (at + FEAT_SUB) // 128):
             part = pl.ds(block * 128, 128)
-            unit = emb_ref[part, :].astype(f32) + rest_ref[part, :].astype(f32)
+            unit = emb_ref[part, :].astype(f32)
             upstream = page_acc[part, :]
             scale = row_to_col(scale_ref[block : block + 1, :], 128)
             inner = jnp.sum(unit * upstream, axis=1, keepdims=True)
@@ -466,14 +437,14 @@
         give_ref[chip, rows, :] = jnp.where(first_core, odd, even).astype(bf16)
 
 
-def backward(core, table, exps, sums, scale, own, other, emb, rest, rows):
+def backward(core, table, exps, sums, scale, own, other, emb, rows):
     vmem = pl.BlockSpec(memory_space=pltpu.VMEM)
     hbm = pl.BlockSpec(memory_space=pltpu.HBM)
     smem = pl.BlockSpec(memory_space=pltpu.SMEM)
     place = pl.BlockSpec(memory_space=pl.ANY)
     return pl.pallas_call(
         backward_kernel,
-        in_specs=[smem, smem, vmem, vmem, vmem, place, place, hbm, hbm, hbm],
+        in_specs=[smem, smem, vmem, vmem, vmem, place, place, vmem, hbm],
         out_specs=[vmem, vmem],
         out_shape=[jax.ShapeDtypeStruct((CHIPS, QROWS + GRAD_PAD, PROJ), bf16)] * 2,
         scratch_shapes=[
@@ -482,30 +453,19 @@
             pltpu.VMEM((P_DEV * TOKP, PROJ), f32),
             pltpu.VMEM((OWNERS * QROWS, PROJ), f32),
             pltpu.VMEM((P_DEV * TOKP, PROJ), bf16),
-            pltpu.VMEM((P_DEV * TOKP, PROJ), bf16),
-            pltpu.VMEM((P_DEV * TOKP, PROJ), bf16),
             pltpu.VMEM((P_DEV * TOKP, D_FEAT), bf16),
             pltpu.VMEM((2, TOKP, LANES), f32),
             pltpu.VMEM((2, TOKP, LANES), bf16),
-            pltpu.SemaphoreType.DMA((FEAT_STEPS + 2,)),
+            pltpu.SemaphoreType.DMA((FEAT_STEPS,)),
             pltpu.SemaphoreType.DMA((2,)),
         ],
-        compiler_params=pltpu.CompilerParams(vmem_limit_bytes=58 * MIB),
+        compiler_params=pltpu.CompilerParams(vmem_limit_bytes=40 * MIB),
         name="backward",
-    )(core, table, exps, sums, scale, own, other, emb, rest, rows)
-
-
-def pair_kernel(a_ref, b_ref, out_ref):
-    out_ref[...] = (a_ref[...].astype(f32) + b_ref[...].astype(f32)).astype(bf16)
+    )(core, table, exps, sums, scale, own, other, emb, rows)
 
 
 def pair_sum(a, b):
-    return pl.pallas_call(
-        pair_kernel,
-        out_shape=jax.ShapeDtypeStruct(a.shape, bf16),
-        compiler_params=SMALL,
-        name="pair_sum",
-    )(a, b)
+    return (a.astype(f32) + b.astype(f32)).astype(bf16)
 
 
 def share_kernel(parts_ref, out_ref):
@@ -590,13 +550,13 @@
     other_core = [(i, i ^ 1) for i in range(OWNERS)]
     core = (lax.axis_index("pages") % 2).astype(i32).reshape(1)
     own = exchange(send_queries(page_ids, queries), "pages", same_core)
-    own, emb, rest, scale = lax.optimization_barrier((own, *project(rows, proj_weight)))
+    own, emb, scale = lax.optimization_barrier((own, *project(rows, proj_weight)))
     other = lax.ppermute(own, "pages", other_core)
     own = own.reshape(CHIPS * QSTRIDE, PROJ)
     other = other.reshape(CHIPS * QSTRIDE, PROJ)
     back, table, exps = forward(core, own, other, emb)
     sums = exchange(back.reshape(OWNERS, SLOTS, 128), "pages")
-    keep, give = backward(core, table, exps, sums, scale, own, other, emb, rest, rows)
+    keep, give = backward(core, table, exps, sums, scale, own, other, emb, rows)
     taken = lax.ppermute(give, "pages", other_core)
     parts = exchange(pair_sum(keep, taken), "pages", same_core)
     share = own_share(parts)

time: 115 us -> 107 us (0.930)
  Pallas kernels: 39.3 us -> 32.2 us
  blocking collectives: 16.2 us -> 13.2 us
  local copies, waits for them, and re-layouts: 3.79 us -> 0.95 us
  waiting for transfers between devices: 27.6 us -> 29.6 us
  starting transfers between devices: 26.5 us -> 28.3 us
    pallas_call x2 -> x1, Pallas kernels: 14.1 us -> 9.84 us  [project(): pl.pallas_call(project_kernel, in_specs=[hbm, vmem], out_specs=[vmem, vme...]
    all_to_all x1, blocking collectives: 16.2 us -> 13.2 us  [exchange(): lax.all_to_all(values, axes, split_axis=0, concat_axis=0, axis_index_grou...]
    all_to_all x3, waiting for transfers between devices: 20.1 us -> 22.2 us  [exchange(): lax.all_to_all(values, axes, split_axis=0, concat_axis=0, axis_index_grou...]
    pallas_call x1, Pallas kernels: 15.1 us -> 12.9 us  [backward(): pl.pallas_call(backward_kernel, in_specs=[smem, smem, vmem, vmem, vmem, p...]
    unnamed x10 -> x6, local copies, waits for them, and re-layouts: 1.95 us -> 0.01 us
  transfers between devices with their start and end apart: 8 -> 8, of which waited for: 6 -> 7; matrix products, arithmetic and copies ran while one was open for 2% -> 1% of each run, Pallas kernels for 12% -> 10%
where the time goes in v4:
time: 107 us
  Pallas kernels  32.2 us (30%)
  waiting for transfers between devices  29.6 us (28%)
  starting transfers between devices  28.3 us (26%)
  blocking collectives  13.2 us (12%)
  other arithmetic  1.56 us (1%)
    all_to_all x3, waiting for transfers between devices, exchange(): lax.all_to_all(values, axes, split_axis=0, concat_axis=0, axis_index_grou...  22.2 us
    all_to_all x3, starting transfers between devices, exchange(): lax.all_to_all(values, axes, split_axis=0, concat_axis=0, axis_index_grou...  20.2 us
    all_to_all x1, blocking collectives, exchange(): lax.all_to_all(values, axes, split_axis=0, concat_axis=0, axis_index_grou...  13.2 us
    pallas_call x1, Pallas kernels, backward(): pl.pallas_call(backward_kernel, in_specs=[smem, smem, vmem, vmem, vmem, p...  12.9 us
    pallas_call x1, Pallas kernels, project(): pl.pallas_call(project_kernel, in_specs=[hbm, vmem], out_specs=[vmem, vme...  9.84 us
    ppermute x3, starting transfers between devices, per_device(): lax.ppermute(share, 'rep', [(i, i ^ k) for i in range(replicas)])  5.54 us
    pallas_call x1, Pallas kernels, forward(): pl.pallas_call(forward_kernel, in_specs=[pl.BlockSpec(memory_space=pltpu....  4.72 us
    ppermute x3, waiting for transfers between devices, per_device(): lax.ppermute(share, 'rep', [(i, i ^ k) for i in range(replicas)])  3.82 us
  transfers between devices with their start and end apart: 8, of which 7 were waited for; matrix products, arithmetic and copies ran while one was open for 1% of the time, Pallas kernels for 10%

profile of v4, /device:TPU:1, one launch (start us, length us, event | category | flops | bytes accessed | tf_op | source)
XLA Modules:
  0.0 106.6 jit_solution(14421153817457426745)
XLA Ops:
  0.6 0.0 copy-start
  0.6 2.2 %send_queries.1 = bf16[16,144,128]{2,1,0:T(8,128)(2,1)} custom-call(s32[4,16]{1,0:T(4,128)} %ids_ref.1, bf16[4,32,128]{2,1,0:T(8,128)(2,1)} %q_ref.3), custom_call_target="tpu_custom_call" | custom-call | tf_op jit(solution)/shard_map/send_queries/pallas_call | solution.py:99
  2.9 7.6 %all-to-all-start = ((bf16[16,144,128]{2,1,0:T(8,128)(2,1)}), bf16[16,144,128]{2,1,0:T(8,128)(2,1)S(1)}, u32[]{:S(2)}, u32[]{:S(2)}) async-start(bf16[16,144,128]{2,1,0:T(8,128)(2,1)} %send_queries.1), calls=%async_computation | async-start | bytes 1179648 | tf_op jit(solution)/shard_map/all_to_all | solution.py:542
  10.5 0.0 copy-done
  10.5 9.8 %project.1 = (bf16[10240,128]{1,0:T(8,128)(2,1)S(1)}, f32[80,128]{1,0:T(8,128)S(1)}) custom-call(bf16[10240,1152]{1,0:T(8,128)(2,1)} %bitcast.9, bf16[1152,128]{1,0:T(8,128)(2,1)S(1)} %copy-done), custom_call_target="tpu_custom_call" | custom-call | flops 3019898880 | bytes 26214400 | tf_op jit(solution)/shard_map/project/pallas_call | solution.py:148
  20.3 1.2 %all-to-all-done = bf16[16,144,128]{2,1,0:T(8,128)(2,1)S(1)} async-done(((bf16[16,144,128]{2,1,0:T(8,128)(2,1)}), bf16[16,144,128]{2,1,0:T(8,128)(2,1)S(1)}, u32[]{:S(2)}, u32[]{:S(2)}) %all-to-all-start) | async-done | bytes 589856 | tf_op jit(solution)/shard_map/all_to_all | solution.py:542
  21.5 2.1 %collective-permute-start = (bf16[16,144,128]{2,1,0:T(8,128)(2,1)S(1)}, bf16[16,144,128]{2,1,0:T(8,128)(2,1)}, u32[]{:S(2)}, u32[]{:S(2)}) collective-permute-start(bf16[16,144,128]{2,1,0:T(8,128)(2,1)S(1)} %all-to-all-done), channel_id=1, source_target_pairs={{0,4},{4,0},{8,12},{12,8},{16,20},{20,16},{24,28},{28,24},{32,36},... | collective-permute-start | bytes 1769480 | tf_op jit(solution)/shard_map/ppermute | solution.py:554
  23.7 1.8 %collective-permute-done = bf16[16,144,128]{2,1,0:T(8,128)(2,1)} collective-permute-done((bf16[16,144,128]{2,1,0:T(8,128)(2,1)S(1)}, bf16[16,144,128]{2,1,0:T(8,128)(2,1)}, u32[]{:S(2)}, u32[]{:S(2)}) %collective-permute-start) | collective-permute-done | bytes 589856 | tf_op jit(solution)/shard_map/ppermute | solution.py:554
  25.4 4.7 %forward.1 = (f32[16,2,8,128]{3,2,1,0:T(8,128)S(1)}, s32[8,640]{1,0:T(8,128)S(1)}, f32[256,128]{1,0:T(8,128)S(1)}) custom-call(s32[1]{0:T(128)} %bitcast.core_ref, bf16[2304,128]{1,0:T(8,128)(2,1)S(1)} %bitcast.6, bf16[2304,128]{1,0:T(8,128)(2,1)} %bitcast.3.other_any, bf16[10240,128]{1,0:T(8,128)(2,1)S(1)} %get-tuple-element.16.emb_ref), custom_call_target="tpu_custom_call" | custom-call | tf_op jit(solution)/shard_map/forward/pallas_call | solution.py:308
  30.1 13.2 %all_to_all.20.sums_ref = f32[32,8,128]{2,1,0:T(8,128)S(1)} all-to-all(f32[32,8,128]{2,1,0:T(8,128)S(1)} %bitcast.8), channel_id=1, replica_groups=mesh['pages'=32,'rep'=4] {'pages'}, dimensions={0} | all-to-all | bytes 262144 | tf_op jit(solution)/shard_map/all_to_all | solution.py:542
  43.3 12.9 %backward.1 = (bf16[16,176,128]{2,1,0:T(8,128)(2,1)S(1)}, bf16[16,176,128]{2,1,0:T(8,128)(2,1)S(1)}) custom-call(s32[1]{0:T(128)} %bitcast.core_ref, s32[8,640]{1,0:T(8,128)S(1)} %get-tuple-element.18.table_ref, f32[256,128]{1,0:T(8,128)S(1)} %get-tuple-element.19.exps_ref, f32[32,8,128]{2,1,0:T(8,128)S(1)} %all_to_all.20.sums_ref, ...), custom_call_target="tpu_custom_call" | custom-call | tf_op jit(solution)/shard_map/backward/pallas_call | solution.py:445
  56.3 0.5 collective-permute-start.1
  56.7 1.8 %collective-permute-done.1 = bf16[16,176,128]{2,1,0:T(8,128)(2,1)S(1)} collective-permute-done((bf16[16,176,128]{2,1,0:T(8,128)(2,1)S(1)}, bf16[16,176,128]{2,1,0:T(8,128)(2,1)S(1)}, u32[]{:S(2)}, u32[]{:S(2)}) %collective-permute-start.1) | collective-permute-done | bytes 720928 | tf_op jit(solution)/shard_map/ppermute | solution.py:560
  58.6 0.0 copy-start.2
  58.6 1.1 add_convert_fusion
  59.6 5.7 %all-to-all-start.2 = ((bf16[16,176,128]{2,1,0:T(8,128)(2,1)}), bf16[16,176,128]{2,1,0:T(8,128)(2,1)S(1)}, u32[]{:S(2)}, u32[]{:S(2)}) async-start(bf16[16,176,128]{2,1,0:T(8,128)(2,1)} %add_convert_fusion), calls=%async_computation.2 | async-start | bytes 1441792 | tf_op jit(solution)/shard_map/all_to_all | solution.py:542
  65.3 0.0 copy-done.2
  65.3 0.0 copy-start.1
  65.4 0.1 div.14
  65.5 0.1 and.31
  65.5 0.1 broadcast_compare_fusion
  65.6 0.1 reduce_window_sum.11
  65.7 12.4 %all-to-all-done.2.parts_ref = bf16[16,176,128]{2,1,0:T(8,128)(2,1)S(1)} async-done(((bf16[16,176,128]{2,1,0:T(8,128)(2,1)}), bf16[16,176,128]{2,1,0:T(8,128)(2,1)S(1)}, u32[]{:S(2)}, u32[]{:S(2)}) %all-to-all-start.2) | async-done | bytes 720928 | tf_op jit(solution)/shard_map/all_to_all | solution.py:542
  78.2 2.2 %collective-permute-start.2 = (f32[48,128]{1,0:T(8,128)S(1)}, f32[48,128]{1,0:T(8,128)S(1)}, u32[]{:S(2)}, u32[]{:S(2)}) collective-permute-start(f32[48,128]{1,0:T(8,128)S(1)} %own_share.1.a_ref), channel_id=1, source_target_pairs={{0,1},{1,0},{2,3},{3,2},{4,5},{5,4},{6,7},{7,6},{8,9},{9,8},{10,11... | collective-permute-start | bytes 73736 | tf_op jit(solution)/shard_map/ppermute | solution.py:565
  80.4 3.3 %collective-permute-start.3 = (f32[48,128]{1,0:T(8,128)S(1)}, f32[48,128]{1,0:T(8,128)S(1)}, u32[]{:S(2)}, u32[]{:S(2)}) collective-permute-start(f32[48,128]{1,0:T(8,128)S(1)} %own_share.1.a_ref), channel_id=1, source_target_pairs={{0,2},{1,3},{2,0},{3,1},{4,6},{5,7},{6,4},{7,5},{8,10},{9,11},{10,... | collective-permute-start | bytes 73736 | tf_op jit(solution)/shard_map/ppermute | solution.py:565
  83.7 0.0 collective-permute-start.4
  83.7 0.2 select_reduce_fusion.1
  83.9 0.0 collective-permute-done.2.b_ref
  83.9 1.3 %collective-permute-done.3.c_ref = f32[48,128]{1,0:T(8,128)S(1)} collective-permute-done((f32[48,128]{1,0:T(8,128)S(1)}, f32[48,128]{1,0:T(8,128)S(1)}, u32[]{:S(2)}, u32[]{:S(2)}) %collective-permute-start.3) | collective-permute-done | bytes 24608 | tf_op jit(solution)/shard_map/ppermute | solution.py:565
  85.2 2.5 %collective-permute-done.4.d_ref = f32[48,128]{1,0:T(8,128)S(1)} collective-permute-done((f32[48,128]{1,0:T(8,128)S(1)}, f32[48,128]{1,0:T(8,128)S(1)}, u32[]{:S(2)}, u32[]{:S(2)}) %collective-permute-start.4) | collective-permute-done | bytes 24608 | tf_op jit(solution)/shard_map/ppermute | solution.py:565
  87.7 0.8 spread_share.1
  88.5 6.9 %all-to-all-start.3 = ((bf16[32,48,128]{2,1,0:T(8,128)(2,1)}), bf16[32,48,128]{2,1,0:T(8,128)(2,1)S(1)}, u32[]{:S(2)}, u32[]{:S(2)}) async-start(bf16[32,48,128]{2,1,0:T(8,128)(2,1)} %spread_share.1), calls=%async_computation.3 | async-start | bytes 786432 | tf_op jit(solution)/shard_map/all_to_all | solution.py:542
  95.4 0.1 copy.7
  95.6 0.1 select_reduce_fusion
  95.7 0.7 reshape.101
  96.3 0.0 copy-done.1
  96.3 0.8 query_grads.1
  97.1 8.6 %all-to-all-done.3.parts_ref = bf16[32,48,128]{2,1,0:T(8,128)(2,1)S(1)} async-done(((bf16[32,48,128]{2,1,0:T(8,128)(2,1)}), bf16[32,48,128]{2,1,0:T(8,128)(2,1)S(1)}, u32[]{:S(2)}, u32[]{:S(2)}) %all-to-all-start.3) | async-done | bytes 393248 | tf_op jit(solution)/shard_map/all_to_all | solution.py:542
  105.7 0.9 collect.1
  (7 shorter events, 0.1 us)
Async XLA Ops:
  0.6 9.8 %copy-start = (bf16[1152,128]{1,0:T(8,128)(2,1)S(1)}, bf16[1152,128]{1,0:T(8,128)(2,1)}, u32[]{:S(2)}) copy-start(bf16[1152,128]{1,0:T(8,128)(2,1)} %w_ref.1) | copy-start | bytes 884740
  2.9 18.7 %all-to-all-start = ((bf16[16,144,128]{2,1,0:T(8,128)(2,1)}), bf16[16,144,128]{2,1,0:T(8,128)(2,1)S(1)}, u32[]{:S(2)}, u32[]{:S(2)}) async-start(bf16[16,144,128]{2,1,0:T(8,128)(2,1)} %send_queries.1), calls=%async_computation | async-start | bytes 1179648 | tf_op jit(solution)/shard_map/all_to_all | solution.py:542
  21.5 3.9 %collective-permute-start = (bf16[16,144,128]{2,1,0:T(8,128)(2,1)S(1)}, bf16[16,144,128]{2,1,0:T(8,128)(2,1)}, u32[]{:S(2)}, u32[]{:S(2)}) collective-permute-start(bf16[16,144,128]{2,1,0:T(8,128)(2,1)S(1)} %all-to-all-done), channel_id=1, source_target_pairs={{0,4},{4,0},{8,12},{12,8},{16,20},{20,16},{24,28},{28,24},{32,36},... | collective-permute-start | bytes 1769480 | tf_op jit(solution)/shard_map/ppermute | solution.py:554
  56.3 2.3 %collective-permute-start.1 = (bf16[16,176,128]{2,1,0:T(8,128)(2,1)S(1)}, bf16[16,176,128]{2,1,0:T(8,128)(2,1)S(1)}, u32[]{:S(2)}, u32[]{:S(2)}) collective-permute-start(bf16[16,176,128]{2,1,0:T(8,128)(2,1)S(1)} %get-tuple-element.22), channel_id=1, source_target_pairs={{0,4},{4,0},{8,12},{12,8},{16,20},{20,16},{24,28},{28,24},{32,36},... | collective-permute-start | bytes 2162696 | tf_op jit(solution)/shard_map/ppermute | solution.py:560
  58.6 6.8 %copy-start.2 = (s32[4,16]{1,0:T(4,128)S(1)}, s32[4,16]{1,0:T(4,128)}, u32[]{:S(2)}) copy-start(s32[4,16]{1,0:T(4,128)} %ids_ref.1) | copy-start | bytes 772
  59.6 18.5 %all-to-all-start.2 = ((bf16[16,176,128]{2,1,0:T(8,128)(2,1)}), bf16[16,176,128]{2,1,0:T(8,128)(2,1)S(1)}, u32[]{:S(2)}, u32[]{:S(2)}) async-start(bf16[16,176,128]{2,1,0:T(8,128)(2,1)} %add_convert_fusion), calls=%async_computation.2 | async-start | bytes 1441792 | tf_op jit(solution)/shard_map/all_to_all | solution.py:542
  65.3 31.0 %copy-start.1 = (bf16[4,32,128]{2,1,0:T(8,128)(2,1)S(1)}, bf16[4,32,128]{2,1,0:T(8,128)(2,1)}, u32[]{:S(2)}) copy-start(bf16[4,32,128]{2,1,0:T(8,128)(2,1)} %q_ref.3) | copy-start | bytes 98308
  78.2 5.7 %collective-permute-start.2 = (f32[48,128]{1,0:T(8,128)S(1)}, f32[48,128]{1,0:T(8,128)S(1)}, u32[]{:S(2)}, u32[]{:S(2)}) collective-permute-start(f32[48,128]{1,0:T(8,128)S(1)} %own_share.1.a_ref), channel_id=1, source_target_pairs={{0,1},{1,0},{2,3},{3,2},{4,5},{5,4},{6,7},{7,6},{8,9},{9,8},{10,11... | collective-permute-start | bytes 73736 | tf_op jit(solution)/shard_map/ppermute | solution.py:565
  80.4 4.8 %collective-permute-start.3 = (f32[48,128]{1,0:T(8,128)S(1)}, f32[48,128]{1,0:T(8,128)S(1)}, u32[]{:S(2)}, u32[]{:S(2)}) collective-permute-start(f32[48,128]{1,0:T(8,128)S(1)} %own_share.1.a_ref), channel_id=1, source_target_pairs={{0,2},{1,3},{2,0},{3,1},{4,6},{5,7},{6,4},{7,5},{8,10},{9,11},{10,... | collective-permute-start | bytes 73736 | tf_op jit(solution)/shard_map/ppermute | solution.py:565
  83.7 4.0 %collective-permute-start.4 = (f32[48,128]{1,0:T(8,128)S(1)}, f32[48,128]{1,0:T(8,128)S(1)}, u32[]{:S(2)}, u32[]{:S(2)}) collective-permute-start(f32[48,128]{1,0:T(8,128)S(1)} %own_share.1.a_ref), channel_id=1, source_target_pairs={{0,3},{1,2},{2,1},{3,0},{4,7},{5,6},{6,5},{7,4},{8,11},{9,10},{10,... | collective-permute-start | bytes 73736 | tf_op jit(solution)/shard_map/ppermute | solution.py:565
  88.5 17.2 %all-to-all-start.3 = ((bf16[32,48,128]{2,1,0:T(8,128)(2,1)}), bf16[32,48,128]{2,1,0:T(8,128)(2,1)S(1)}, u32[]{:S(2)}, u32[]{:S(2)}) async-start(bf16[32,48,128]{2,1,0:T(8,128)(2,1)} %spread_share.1), calls=%async_computation.3 | async-start | bytes 786432 | tf_op jit(solution)/shard_map/all_to_all | solution.py:542

commit v5 on v4

--- a/solution.py
+++ b/solution.py
@@ -333,7 +333,7 @@
 
 
 FEAT_STEPS = 5
-FEAT_SUB = 1024
+FEAT_SUB = 512
 FEAT_ROWS = P_DEV * TOKP // FEAT_STEPS
 
 
@@ -353,6 +353,8 @@
     grads_ref[...] = jnp.zeros(grads_ref.shape, bf16)
     for copy in received:
         copy.wait()
+    for step in range(FEAT_STEPS):
+        feature_copy(step).start()
     page, query, of_source, positive = slot_columns(recv_ref, core_ref[0])
     sums = jnp.sum(sums_ref[...], axis=0)[0:1]
     lane = iota((ENTRIES, 128), 1)
@@ -363,8 +365,6 @@
         valid, exps_ref[...] / total - positive.astype(f32), 0.0
     )
     weight_of[ENTRIES : ENTRIES + 8, :] = jnp.zeros((8, 128), f32)
-    for step in range(FEAT_STEPS):
-        feature_copy(step).start()
     group = iota((1, 128), 1) // QTOK
 
     def chunk_weights(chunk):

time: 107 us -> 107 us (level)
  Pallas kernels: 32.2 us -> 33.3 us
where the time goes in v5:
time: 107 us
  Pallas kernels  33.3 us (31%)
  waiting for transfers between devices  29.6 us (28%)
  starting transfers between devices  27.6 us (26%)
  blocking collectives  13.1 us (12%)
  other arithmetic  1.56 us (1%)
    all_to_all x3, waiting for transfers between devices, exchange(): lax.all_to_all(values, axes, split_axis=0, concat_axis=0, axis_index_grou...  22.2 us
    all_to_all x3, starting transfers between devices, exchange(): lax.all_to_all(values, axes, split_axis=0, concat_axis=0, axis_index_grou...  20 us
    pallas_call x1, Pallas kernels, backward(): pl.pallas_call(backward_kernel, in_specs=[smem, smem, vmem, vmem, vmem, p...  13.6 us
    all_to_all x1, blocking collectives, exchange(): lax.all_to_all(values, axes, split_axis=0, concat_axis=0, axis_index_grou...  13.1 us
    pallas_call x1, Pallas kernels, project(): pl.pallas_call(project_kernel, in_specs=[hbm, vmem], out_specs=[vmem, vme...  9.84 us
    pallas_call x1, Pallas kernels, forward(): pl.pallas_call(forward_kernel, in_specs=[pl.BlockSpec(memory_space=pltpu....  5.19 us
    ppermute x3, starting transfers between devices, per_device(): lax.ppermute(share, 'rep', [(i, i ^ k) for i in range(replicas)])  5.02 us
    ppermute x3, waiting for transfers between devices, per_device(): lax.ppermute(share, 'rep', [(i, i ^ k) for i in range(replicas)])  3.82 us
  transfers between devices with their start and end apart: 8, of which 7 were waited for; matrix products, arithmetic and copies ran while one was open for 1% of the time, Pallas kernels for 10%

profile of v5, /device:TPU:1, one launch (start us, length us, event | category | flops | bytes accessed | tf_op | source)
XLA Modules:
  0.0 107.0 jit_solution(17736789304256405847)
XLA Ops:
  0.6 0.0 copy-start
  0.6 2.2 %send_queries.1 = bf16[16,144,128]{2,1,0:T(8,128)(2,1)} custom-call(s32[4,16]{1,0:T(4,128)} %ids_ref.1, bf16[4,32,128]{2,1,0:T(8,128)(2,1)} %q_ref.3), custom_call_target="tpu_custom_call" | custom-call | tf_op jit(solution)/shard_map/send_queries/pallas_call | solution.py:99
  2.9 7.6 %all-to-all-start = ((bf16[16,144,128]{2,1,0:T(8,128)(2,1)}), bf16[16,144,128]{2,1,0:T(8,128)(2,1)S(1)}, u32[]{:S(2)}, u32[]{:S(2)}) async-start(bf16[16,144,128]{2,1,0:T(8,128)(2,1)} %send_queries.1), calls=%async_computation | async-start | bytes 1179648 | tf_op jit(solution)/shard_map/all_to_all | solution.py:542
  10.5 0.0 copy-done
  10.5 9.8 %project.1 = (bf16[10240,128]{1,0:T(8,128)(2,1)S(1)}, f32[80,128]{1,0:T(8,128)S(1)}) custom-call(bf16[10240,1152]{1,0:T(8,128)(2,1)} %bitcast.9, bf16[1152,128]{1,0:T(8,128)(2,1)S(1)} %copy-done), custom_call_target="tpu_custom_call" | custom-call | flops 3019898880 | bytes 26214400 | tf_op jit(solution)/shard_map/project/pallas_call | solution.py:148
  20.3 1.2 %all-to-all-done = bf16[16,144,128]{2,1,0:T(8,128)(2,1)S(1)} async-done(((bf16[16,144,128]{2,1,0:T(8,128)(2,1)}), bf16[16,144,128]{2,1,0:T(8,128)(2,1)S(1)}, u32[]{:S(2)}, u32[]{:S(2)}) %all-to-all-start) | async-done | bytes 589856 | tf_op jit(solution)/shard_map/all_to_all | solution.py:542
  21.5 2.1 %collective-permute-start = (bf16[16,144,128]{2,1,0:T(8,128)(2,1)S(1)}, bf16[16,144,128]{2,1,0:T(8,128)(2,1)}, u32[]{:S(2)}, u32[]{:S(2)}) collective-permute-start(bf16[16,144,128]{2,1,0:T(8,128)(2,1)S(1)} %all-to-all-done), channel_id=1, source_target_pairs={{0,4},{4,0},{8,12},{12,8},{16,20},{20,16},{24,28},{28,24},{32,36},... | collective-permute-start | bytes 1769480 | tf_op jit(solution)/shard_map/ppermute | solution.py:554
  23.7 1.8 %collective-permute-done = bf16[16,144,128]{2,1,0:T(8,128)(2,1)} collective-permute-done((bf16[16,144,128]{2,1,0:T(8,128)(2,1)S(1)}, bf16[16,144,128]{2,1,0:T(8,128)(2,1)}, u32[]{:S(2)}, u32[]{:S(2)}) %collective-permute-start) | collective-permute-done | bytes 589856 | tf_op jit(solution)/shard_map/ppermute | solution.py:554
  25.4 5.2 %forward.1 = (f32[16,2,8,128]{3,2,1,0:T(8,128)S(1)}, s32[8,640]{1,0:T(8,128)S(1)}, f32[256,128]{1,0:T(8,128)S(1)}) custom-call(s32[1]{0:T(128)} %bitcast.core_ref, bf16[2304,128]{1,0:T(8,128)(2,1)S(1)} %bitcast.6, bf16[2304,128]{1,0:T(8,128)(2,1)} %bitcast.3.other_any, bf16[10240,128]{1,0:T(8,128)(2,1)S(1)} %get-tuple-element.16.emb_ref), custom_call_target="tpu_custom_call" | custom-call | tf_op jit(solution)/shard_map/forward/pallas_call | solution.py:308
  30.6 13.1 %all_to_all.20.sums_ref = f32[32,8,128]{2,1,0:T(8,128)S(1)} all-to-all(f32[32,8,128]{2,1,0:T(8,128)S(1)} %bitcast.8), channel_id=1, replica_groups=mesh['pages'=32,'rep'=4] {'pages'}, dimensions={0} | all-to-all | bytes 262144 | tf_op jit(solution)/shard_map/all_to_all | solution.py:542
  43.8 13.6 %backward.1 = (bf16[16,176,128]{2,1,0:T(8,128)(2,1)S(1)}, bf16[16,176,128]{2,1,0:T(8,128)(2,1)S(1)}) custom-call(s32[1]{0:T(128)} %bitcast.core_ref, s32[8,640]{1,0:T(8,128)S(1)} %get-tuple-element.18.table_ref, f32[256,128]{1,0:T(8,128)S(1)} %get-tuple-element.19.exps_ref, f32[32,8,128]{2,1,0:T(8,128)S(1)} %all_to_all.20.sums_ref, ...), custom_call_target="tpu_custom_call" | custom-call | tf_op jit(solution)/shard_map/backward/pallas_call | solution.py:445
  57.4 0.5 collective-permute-start.1
  57.9 1.8 %collective-permute-done.1 = bf16[16,176,128]{2,1,0:T(8,128)(2,1)S(1)} collective-permute-done((bf16[16,176,128]{2,1,0:T(8,128)(2,1)S(1)}, bf16[16,176,128]{2,1,0:T(8,128)(2,1)S(1)}, u32[]{:S(2)}, u32[]{:S(2)}) %collective-permute-start.1) | collective-permute-done | bytes 720928 | tf_op jit(solution)/shard_map/ppermute | solution.py:560
  59.7 0.0 copy-start.2
  59.7 1.1 add_convert_fusion
  60.8 5.5 %all-to-all-start.2 = ((bf16[16,176,128]{2,1,0:T(8,128)(2,1)}), bf16[16,176,128]{2,1,0:T(8,128)(2,1)S(1)}, u32[]{:S(2)}, u32[]{:S(2)}) async-start(bf16[16,176,128]{2,1,0:T(8,128)(2,1)} %add_convert_fusion), calls=%async_computation.2 | async-start | bytes 1441792 | tf_op jit(solution)/shard_map/all_to_all | solution.py:542
  66.2 0.0 copy-done.2
  66.2 0.0 copy-start.1
  66.3 0.1 div.14
  66.4 0.1 and.31
  66.5 0.1 broadcast_compare_fusion
  66.6 0.1 reduce_window_sum.11
  66.7 12.4 %all-to-all-done.2.parts_ref = bf16[16,176,128]{2,1,0:T(8,128)(2,1)S(1)} async-done(((bf16[16,176,128]{2,1,0:T(8,128)(2,1)}), bf16[16,176,128]{2,1,0:T(8,128)(2,1)S(1)}, u32[]{:S(2)}, u32[]{:S(2)}) %all-to-all-start.2) | async-done | bytes 720928 | tf_op jit(solution)/shard_map/all_to_all | solution.py:542
  79.1 1.7 %collective-permute-start.2 = (f32[48,128]{1,0:T(8,128)S(1)}, f32[48,128]{1,0:T(8,128)S(1)}, u32[]{:S(2)}, u32[]{:S(2)}) collective-permute-start(f32[48,128]{1,0:T(8,128)S(1)} %own_share.1.a_ref), channel_id=1, source_target_pairs={{0,1},{1,0},{2,3},{3,2},{4,5},{5,4},{6,7},{7,6},{8,9},{9,8},{10,11... | collective-permute-start | bytes 73736 | tf_op jit(solution)/shard_map/ppermute | solution.py:565
  80.7 3.4 %collective-permute-start.3 = (f32[48,128]{1,0:T(8,128)S(1)}, f32[48,128]{1,0:T(8,128)S(1)}, u32[]{:S(2)}, u32[]{:S(2)}) collective-permute-start(f32[48,128]{1,0:T(8,128)S(1)} %own_share.1.a_ref), channel_id=1, source_target_pairs={{0,2},{1,3},{2,0},{3,1},{4,6},{5,7},{6,4},{7,5},{8,10},{9,11},{10,... | collective-permute-start | bytes 73736 | tf_op jit(solution)/shard_map/ppermute | solution.py:565
  84.1 0.0 collective-permute-start.4
  84.1 0.2 select_reduce_fusion.1
  84.3 0.0 collective-permute-done.2.b_ref
  84.3 1.3 %collective-permute-done.3.c_ref = f32[48,128]{1,0:T(8,128)S(1)} collective-permute-done((f32[48,128]{1,0:T(8,128)S(1)}, f32[48,128]{1,0:T(8,128)S(1)}, u32[]{:S(2)}, u32[]{:S(2)}) %collective-permute-start.3) | collective-permute-done | bytes 24608 | tf_op jit(solution)/shard_map/ppermute | solution.py:565
  85.6 2.5 %collective-permute-done.4.d_ref = f32[48,128]{1,0:T(8,128)S(1)} collective-permute-done((f32[48,128]{1,0:T(8,128)S(1)}, f32[48,128]{1,0:T(8,128)S(1)}, u32[]{:S(2)}, u32[]{:S(2)}) %collective-permute-start.4) | collective-permute-done | bytes 24608 | tf_op jit(solution)/shard_map/ppermute | solution.py:565
  88.1 0.8 spread_share.1
  88.9 6.9 %all-to-all-start.3 = ((bf16[32,48,128]{2,1,0:T(8,128)(2,1)}), bf16[32,48,128]{2,1,0:T(8,128)(2,1)S(1)}, u32[]{:S(2)}, u32[]{:S(2)}) async-start(bf16[32,48,128]{2,1,0:T(8,128)(2,1)} %spread_share.1), calls=%async_computation.3 | async-start | bytes 786432 | tf_op jit(solution)/shard_map/all_to_all | solution.py:542
  95.8 0.1 copy.7
  95.9 0.1 select_reduce_fusion
  96.1 0.7 reshape.101
  96.7 0.0 copy-done.1
  96.7 0.8 query_grads.1
  97.5 8.6 %all-to-all-done.3.parts_ref = bf16[32,48,128]{2,1,0:T(8,128)(2,1)S(1)} async-done(((bf16[32,48,128]{2,1,0:T(8,128)(2,1)}), bf16[32,48,128]{2,1,0:T(8,128)(2,1)S(1)}, u32[]{:S(2)}, u32[]{:S(2)}) %all-to-all-start.3) | async-done | bytes 393248 | tf_op jit(solution)/shard_map/all_to_all | solution.py:542
  106.1 0.9 collect.1
  (7 shorter events, 0.1 us)
Async XLA Ops:
  0.6 9.8 %copy-start = (bf16[1152,128]{1,0:T(8,128)(2,1)S(1)}, bf16[1152,128]{1,0:T(8,128)(2,1)}, u32[]{:S(2)}) copy-start(bf16[1152,128]{1,0:T(8,128)(2,1)} %w_ref.1) | copy-start | bytes 884740
  2.9 18.7 %all-to-all-start = ((bf16[16,144,128]{2,1,0:T(8,128)(2,1)}), bf16[16,144,128]{2,1,0:T(8,128)(2,1)S(1)}, u32[]{:S(2)}, u32[]{:S(2)}) async-start(bf16[16,144,128]{2,1,0:T(8,128)(2,1)} %send_queries.1), calls=%async_computation | async-start | bytes 1179648 | tf_op jit(solution)/shard_map/all_to_all | solution.py:542
  21.5 3.9 %collective-permute-start = (bf16[16,144,128]{2,1,0:T(8,128)(2,1)S(1)}, bf16[16,144,128]{2,1,0:T(8,128)(2,1)}, u32[]{:S(2)}, u32[]{:S(2)}) collective-permute-start(bf16[16,144,128]{2,1,0:T(8,128)(2,1)S(1)} %all-to-all-done), channel_id=1, source_target_pairs={{0,4},{4,0},{8,12},{12,8},{16,20},{20,16},{24,28},{28,24},{32,36},... | collective-permute-start | bytes 1769480 | tf_op jit(solution)/shard_map/ppermute | solution.py:554
  57.4 2.3 %collective-permute-start.1 = (bf16[16,176,128]{2,1,0:T(8,128)(2,1)S(1)}, bf16[16,176,128]{2,1,0:T(8,128)(2,1)S(1)}, u32[]{:S(2)}, u32[]{:S(2)}) collective-permute-start(bf16[16,176,128]{2,1,0:T(8,128)(2,1)S(1)} %get-tuple-element.22), channel_id=1, source_target_pairs={{0,4},{4,0},{8,12},{12,8},{16,20},{20,16},{24,28},{28,24},{32,36},... | collective-permute-start | bytes 2162696 | tf_op jit(solution)/shard_map/ppermute | solution.py:560
  59.7 6.5 %copy-start.2 = (s32[4,16]{1,0:T(4,128)S(1)}, s32[4,16]{1,0:T(4,128)}, u32[]{:S(2)}) copy-start(s32[4,16]{1,0:T(4,128)} %ids_ref.1) | copy-start | bytes 772
  60.8 18.3 %all-to-all-start.2 = ((bf16[16,176,128]{2,1,0:T(8,128)(2,1)}), bf16[16,176,128]{2,1,0:T(8,128)(2,1)S(1)}, u32[]{:S(2)}, u32[]{:S(2)}) async-start(bf16[16,176,128]{2,1,0:T(8,128)(2,1)} %add_convert_fusion), calls=%async_computation.2 | async-start | bytes 1441792 | tf_op jit(solution)/shard_map/all_to_all | solution.py:542
  66.2 30.5 %copy-start.1 = (bf16[4,32,128]{2,1,0:T(8,128)(2,1)S(1)}, bf16[4,32,128]{2,1,0:T(8,128)(2,1)}, u32[]{:S(2)}) copy-start(bf16[4,32,128]{2,1,0:T(8,128)(2,1)} %q_ref.3) | copy-start | bytes 98308
  79.1 5.2 %collective-permute-start.2 = (f32[48,128]{1,0:T(8,128)S(1)}, f32[48,128]{1,0:T(8,128)S(1)}, u32[]{:S(2)}, u32[]{:S(2)}) collective-permute-start(f32[48,128]{1,0:T(8,128)S(1)} %own_share.1.a_ref), channel_id=1, source_target_pairs={{0,1},{1,0},{2,3},{3,2},{4,5},{5,4},{6,7},{7,6},{8,9},{9,8},{10,11... | collective-permute-start | bytes 73736 | tf_op jit(solution)/shard_map/ppermute | solution.py:565
  80.7 4.8 %collective-permute-start.3 = (f32[48,128]{1,0:T(8,128)S(1)}, f32[48,128]{1,0:T(8,128)S(1)}, u32[]{:S(2)}, u32[]{:S(2)}) collective-permute-start(f32[48,128]{1,0:T(8,128)S(1)} %own_share.1.a_ref), channel_id=1, source_target_pairs={{0,2},{1,3},{2,0},{3,1},{4,6},{5,7},{6,4},{7,5},{8,10},{9,11},{10,... | collective-permute-start | bytes 73736 | tf_op jit(solution)/shard_map/ppermute | solution.py:565
  84.1 4.0 %collective-permute-start.4 = (f32[48,128]{1,0:T(8,128)S(1)}, f32[48,128]{1,0:T(8,128)S(1)}, u32[]{:S(2)}, u32[]{:S(2)}) collective-permute-start(f32[48,128]{1,0:T(8,128)S(1)} %own_share.1.a_ref), channel_id=1, source_target_pairs={{0,3},{1,2},{2,1},{3,0},{4,7},{5,6},{6,5},{7,4},{8,11},{9,10},{10,... | collective-permute-start | bytes 73736 | tf_op jit(solution)/shard_map/ppermute | solution.py:565
  88.9 17.2 %all-to-all-start.3 = ((bf16[32,48,128]{2,1,0:T(8,128)(2,1)}), bf16[32,48,128]{2,1,0:T(8,128)(2,1)S(1)}, u32[]{:S(2)}, u32[]{:S(2)}) async-start(bf16[32,48,128]{2,1,0:T(8,128)(2,1)} %spread_share.1), calls=%async_computation.3 | async-start | bytes 786432 | tf_op jit(solution)/shard_map/all_to_all | solution.py:542
